TPU v7x, 256 devices: a whole 4x4x8 slice. The times are simulated.
256 devices in a mesh: seq: 256 (over x, y, z, core).
Axes of the slice: x: 4, y: 4, z: 8, core: 2. Of those that a mesh axis runs over, the one named last changes fastest.
Arguments:
- queries: bfloat16 [40960, 1024], P('seq'), may hold values from -8 to 8
- key_rows: bfloat16 [40960, 1024], P('seq'), may hold values from -8 to 8
- value_rows: bfloat16 [40960, 1024], P('seq'), may hold values from -6 to 6
- out_weight: bfloat16 [1048576], P('seq'), may hold values from -0.75 to 0.75
- cotangent: bfloat16 [40960, 1024], P('seq'), may hold values from -6 to 6
- row_lengths: int32 [204], replicated, may hold values from 1 to 400, 40960 in all
- window_shift: int32 [40960], P('seq'), may hold values from 0 to 720
Outputs:
- layer_out: bfloat16 [40960, 1024], P('seq')
- grad_queries: bfloat16 [40960, 1024], P('seq')
- grad_keys: bfloat16 [40960, 1024], P('seq')
- grad_values: bfloat16 [40960, 1024], P('seq')
- grad_weight: float32 [1048576], P('seq')
All inputs are finite; a program needn't handle non-finite values.
Results may differ from a plain program's by a relative error of at most 0.025.
Values may be sent and summed in bfloat16 or wider, within the bound.
A program may use at most 128 MiB of HBM per device.

v0:
```python
import math

import jax
import jax.numpy as jnp
from jax import lax
from jax.sharding import PartitionSpec as P

D = 1024
HEADS = 16
HEAD = 64
WIN = 1120


def as_sent(shard):

    def short(part):
        return part.astype(jnp.bfloat16) if part.dtype == jnp.float32 else part

    return jax.tree.map(short, shard)


def passed_along(block, axis, distance):
    devices = range(lax.axis_size(axis))
    route = [(i - distance, i) for i in devices if i - distance in devices]
    return lax.ppermute(block, axis, route)


def head_view(block):
    return block.reshape(block.shape[0], -1, HEAD)


def window_starts(row_lengths, window_shift, first_point, all_points):
    point_index = first_point + jnp.arange(window_shift.shape[0], dtype=jnp.int32)
    row_ends = jnp.cumsum(row_lengths)
    passed = row_ends[None, :] <= point_index[:, None]
    row_first = jnp.sum(jnp.where(passed, row_lengths[None, :], 0), axis=1)
    return jnp.clip(row_first - window_shift, 0, all_points - WIN)


def join_rows(pieces):
    return jax.tree.map(lambda *blocks: jnp.concatenate(blocks, 0), *pieces)


def stacked_rims(payload, shifter, rim_reach):
    lower_rims = join_rows([shifter(payload, distance) for distance in range(rim_reach, 0, -1)])
    upper_rims = join_rows([shifter(payload, -distance) for distance in range(1, rim_reach + 1)])
    return join_rows([lower_rims, payload, upper_rims])


def move_keys(payload, distance):
    return jax.tree.map(
        lambda part, own: part.astype(own.dtype),
        passed_along(as_sent(payload), "seq", distance),
        payload,
    )


def move_queries(payload, distance):
    return jax.tree.map(
        lambda part, own: part.astype(own.dtype),
        passed_along(as_sent(payload), "seq", distance),
        payload,
    )


def move_stats(payload, distance):
    return passed_along(payload, "seq", distance)


def column_slice(block, group_index, group_cols):
    return head_view(lax.dynamic_slice_in_dim(block, group_index * group_cols, group_cols, 1))


def head_pair(table, group_index):
    return lax.dynamic_slice_in_dim(table, group_index * 2, 2, 1).T[:, :, None]


def per_device(queries, key_rows, value_rows, out_weight, cotangent, row_lengths, window_shift):
    point_rows = queries.shape[0]
    devices = lax.axis_size("seq")
    all_points = point_rows * devices
    rim_reach = (WIN - 2 + point_rows) // point_rows
    rim_rows = (2 * rim_reach + 1) * point_rows
    head_scale = 1.0 / math.sqrt(HEAD)
    group_cols = 2 * HEAD
    groups = HEADS // 2
    group_list = jnp.arange(groups, dtype=jnp.int32)
    first_point = lax.axis_index("seq") * point_rows
    starts = window_starts(row_lengths, window_shift, first_point, all_points)
    rim_index = first_point - rim_reach * point_rows + jnp.arange(rim_rows, dtype=jnp.int32)
    own_index = first_point + jnp.arange(point_rows, dtype=jnp.int32)
    allowed = (rim_index[None, :] >= starts[:, None]) & (rim_index[None, :] < starts[:, None] + WIN)
    gathered = lax.all_gather(out_weight, "seq", axis=0, tiled=True).reshape(D, D)
    key_rims, value_rims = stacked_rims((key_rows, value_rows), move_keys, rim_reach)

    def forward_group(group_index):
        query_part = column_slice(queries, group_index, group_cols)
        key_part = column_slice(key_rims, group_index, group_cols)
        value_part = column_slice(value_rims, group_index, group_cols)
        scores = (
            jnp.einsum("qhd,khd->hqk", query_part, key_part, preferred_element_type=jnp.float32)
            * head_scale
        )
        scores = jnp.where(allowed[None], scores, -jnp.inf)
        row_top = jnp.max(scores, axis=2, keepdims=True)
        log_total = row_top + jnp.log(jnp.sum(jnp.exp(scores - row_top), axis=2, keepdims=True))
        softmax_out = jnp.exp(scores - log_total).astype(jnp.bfloat16)
        mixed = jnp.einsum(
            "hqk,khd->qhd", softmax_out, value_part, preferred_element_type=jnp.float32
        )
        return (mixed.reshape(point_rows, group_cols).astype(jnp.bfloat16), log_total[:, :, 0])

    mixed_groups, total_groups = lax.map(forward_group, group_list)
    mixed = jnp.transpose(mixed_groups, (1, 0, 2)).reshape(point_rows, D)
    log_total = total_groups.reshape(HEADS, point_rows).T
    layer_out = jnp.dot(mixed, gathered, preferred_element_type=jnp.float32).astype(jnp.bfloat16)
    grad_mixed = lax.dot_general(
        cotangent, gathered, (((1,), (1,)), ((), ())), preferred_element_type=jnp.float32
    ).astype(jnp.bfloat16)
    row_delta = jnp.sum(
        (grad_mixed.astype(jnp.float32) * mixed.astype(jnp.float32)).reshape(
            point_rows, HEADS, HEAD
        ),
        axis=2,
    )
    weight_term = lax.dot_general(
        mixed, cotangent, (((0,), (0,)), ((), ())), preferred_element_type=jnp.float32
    ) * (1.0 / math.sqrt(all_points))
    grad_weight = lax.psum_scatter(
        weight_term.reshape(D * D), "seq", scatter_dimension=0, tiled=True
    )

    def query_group(group_index):
        query_part = column_slice(queries, group_index, group_cols)
        key_part = column_slice(key_rims, group_index, group_cols)
        value_part = column_slice(value_rims, group_index, group_cols)
        grad_part = column_slice(grad_mixed, group_index, group_cols)
        scores = (
            jnp.einsum("qhd,khd->hqk", query_part, key_part, preferred_element_type=jnp.float32)
            * head_scale
        )
        scores = jnp.where(allowed[None], scores, -jnp.inf)
        chances = jnp.exp(scores - head_pair(log_total, group_index))
        grad_scores = jnp.einsum(
            "qhd,khd->hqk", grad_part, value_part, preferred_element_type=jnp.float32
        )
        slopes = (chances * (grad_scores - head_pair(row_delta, group_index))).astype(jnp.bfloat16)
        grad_query = (
            jnp.einsum("hqk,khd->qhd", slopes, key_part, preferred_element_type=jnp.float32)
            * head_scale
        )
        return grad_query.reshape(point_rows, group_cols).astype(jnp.bfloat16)

    grad_queries = jnp.transpose(lax.map(query_group, group_list), (1, 0, 2)).reshape(point_rows, D)
    query_rims, grad_rims = stacked_rims((queries, grad_mixed), move_queries, rim_reach)
    total_rims, delta_rims, start_rims = stacked_rims(
        (log_total, row_delta, starts.astype(jnp.float32)), move_stats, rim_reach
    )
    rim_starts = start_rims.astype(jnp.int32)
    in_range = (rim_index >= 0) & (rim_index < all_points)
    allowed_back = (
        in_range[:, None]
        & (own_index[None, :] >= rim_starts[:, None])
        & (own_index[None, :] < rim_starts[:, None] + WIN)
    )

    def key_group(group_index):
        query_part = column_slice(query_rims, group_index, group_cols)
        grad_part = column_slice(grad_rims, group_index, group_cols)
        key_part = column_slice(key_rows, group_index, group_cols)
        value_part = column_slice(value_rows, group_index, group_cols)
        scores = (
            jnp.einsum("qhd,khd->hqk", query_part, key_part, preferred_element_type=jnp.float32)
            * head_scale
        )
        scores = jnp.where(allowed_back[None], scores, -jnp.inf)
        chances = jnp.exp(scores - head_pair(total_rims, group_index))
        grad_scores = jnp.einsum(
            "qhd,khd->hqk", grad_part, value_part, preferred_element_type=jnp.float32
        )
        slopes = (chances * (grad_scores - head_pair(delta_rims, group_index))).astype(jnp.bfloat16)
        grad_key = (
            jnp.einsum("hqk,qhd->khd", slopes, query_part, preferred_element_type=jnp.float32)
            * head_scale
        )
        grad_value = jnp.einsum(
            "hqk,qhd->khd",
            chances.astype(jnp.bfloat16),
            grad_part,
            preferred_element_type=jnp.float32,
        )
        return (
            grad_key.reshape(point_rows, group_cols).astype(jnp.bfloat16),
            grad_value.reshape(point_rows, group_cols).astype(jnp.bfloat16),
        )

    key_groups, value_groups = lax.map(key_group, group_list)
    grad_keys = jnp.transpose(key_groups, (1, 0, 2)).reshape(point_rows, D)
    grad_values = jnp.transpose(value_groups, (1, 0, 2)).reshape(point_rows, D)
    return (layer_out, grad_queries, grad_keys, grad_values, grad_weight)


def solution(mesh):
    return jax.shard_map(
        per_device,
        mesh=mesh,
        in_specs=(
            P("seq", None),
            P("seq", None),
            P("seq", None),
            P("seq"),
            P("seq", None),
            P(),
            P("seq"),
        ),
        out_specs=(P("seq", None), P("seq", None), P("seq", None), P("seq", None), P("seq")),
        check_vma=False,
    )
```

profile of v0, /device:TPU:25, one launch (start us, length us, event | category | flops | bytes accessed | tf_op | source)
XLA Modules:
  0.0 1486.4 jit_solution(14656729600326019152)
XLA Ops:
  33.8 31.3 %collective-permute-done = bf16[160,1024]{0,1:T(8,128)(2,1)S(1)} collective-permute-done((bf16[160,1024]{0,1:T(8,128)(2,1)}, bf16[160,1024]{0,1:T(8,128)(2,1)S(1)}, u32[]{:S(2)}, u32[]{:S(2)}) %collective-permute-start) | collective-permute-done | bytes 327712 | tf_op jit(solution)/shard_map/ppermute | solution.py:25
  67.0 14.0 collective-permute-done.1
  81.0 22.0 %collective-permute-start.6 = (bf16[160,1024]{0,1:T(8,128)(2,1)}, bf16[160,1024]{0,1:T(8,128)(2,1)}, u32[]{:S(2)}, u32[]{:S(2)}) collective-permute-start(bf16[160,1024]{0,1:T(8,128)(2,1)} %copy.233), channel_id=1, source_target_pairs={{0,1},{1,2},{2,3},{3,4},{4,5},{5,6},{6,7},{7,8},{8,9},{9,10},{10,1... | collective-permute-start | bytes 983048 | tf_op jit(solution)/shard_map/ppermute | solution.py:25
  116.4 16.6 %collective-permute-start.8 = (bf16[160,1024]{0,1:T(8,128)(2,1)}, bf16[160,1024]{0,1:T(8,128)(2,1)S(1)}, u32[]{:S(2)}, u32[]{:S(2)}) collective-permute-start(bf16[160,1024]{0,1:T(8,128)(2,1)} %copy.233), channel_id=1, source_target_pairs={{2,0},{3,1},{4,2},{5,3},{6,4},{7,5},{8,6},{9,7},{10,8},{11,9},{12,... | collective-permute-start | bytes 983048 | tf_op jit(solution)/shard_map/ppermute | solution.py:25
  133.1 19.5 %collective-permute-done.4 = bf16[160,1024]{0,1:T(8,128)(2,1)S(1)} collective-permute-done((bf16[160,1024]{0,1:T(8,128)(2,1)}, bf16[160,1024]{0,1:T(8,128)(2,1)S(1)}, u32[]{:S(2)}, u32[]{:S(2)}) %collective-permute-start.4) | collective-permute-done | bytes 327712 | tf_op jit(solution)/shard_map/ppermute | solution.py:25
  207.3 24.4 %collective-permute-done.11 = bf16[160,1024]{0,1:T(8,128)(2,1)} collective-permute-done((bf16[160,1024]{0,1:T(8,128)(2,1)}, bf16[160,1024]{0,1:T(8,128)(2,1)}, u32[]{:S(2)}, u32[]{:S(2)}) %collective-permute-start.11) | collective-permute-done | bytes 327712 | tf_op jit(solution)/shard_map/ppermute | solution.py:25
  233.5 33.6 %collective-permute-done.12 = bf16[160,1024]{0,1:T(8,128)(2,1)} collective-permute-done((bf16[160,1024]{0,1:T(8,128)(2,1)}, bf16[160,1024]{0,1:T(8,128)(2,1)}, u32[]{:S(2)}, u32[]{:S(2)}) %collective-permute-start.12) | collective-permute-done | bytes 327712 | tf_op jit(solution)/shard_map/ppermute | solution.py:25
  269.1 31.1 %collective-permute-done.13 = bf16[160,1024]{0,1:T(8,128)(2,1)S(1)} collective-permute-done((bf16[160,1024]{0,1:T(8,128)(2,1)}, bf16[160,1024]{0,1:T(8,128)(2,1)S(1)}, u32[]{:S(2)}, u32[]{:S(2)}) %collective-permute-start.13) | collective-permute-done | bytes 327712 | tf_op jit(solution)/shard_map/ppermute | solution.py:25
  319.8 14.8 collective-permute-done.18
  378.7 46.4 %collective-permute-done.25 = bf16[160,1024]{0,1:T(8,128)(2,1)} collective-permute-done((bf16[160,1024]{0,1:T(8,128)(2,1)}, bf16[160,1024]{0,1:T(8,128)(2,1)}, u32[]{:S(2)}, u32[]{:S(2)}) %collective-permute-start.25) | collective-permute-done | bytes 327712 | tf_op jit(solution)/shard_map/ppermute | solution.py:25
  425.1 13.4 collective-permute-done.26
  438.5 20.0 %collective-permute-done.27 = bf16[160,1024]{0,1:T(8,128)(2,1)} collective-permute-done((bf16[160,1024]{0,1:T(8,128)(2,1)}, bf16[160,1024]{0,1:T(8,128)(2,1)}, u32[]{:S(2)}, u32[]{:S(2)}) %collective-permute-start.27) | collective-permute-done | bytes 327712 | tf_op jit(solution)/shard_map/ppermute | solution.py:25
  469.2 49.2 %while.37 = (s32[]{:T(128)}, bf16[8,160,128]{1,2,0:T(8,128)(2,1)S(1)}, f32[8,2,160]{2,1,0:T(2,128)S(1)}, s32[8]{0:T(128)S(1)}, bf16[2400,1024]{0,1:T(8,128)(2,1)...) while((s32[]{:T(128)}, ...), condition=%wide.region_6.7_spmd.clone, body=%wide.region_3.6_spmd.clone.sunk | while | flops 203156160 | bytes 13989719 | solution.py:113
  522.2 14.5 collective-permute-start.28
  538.6 12.8 collective-permute-start.30
  556.8 96.8 %collective-permute-done.42 = f32[160]{0:T(256)S(1)} collective-permute-done((f32[160]{0:T(256)S(1)}, f32[160]{0:T(256)S(1)}, u32[]{:S(2)}, u32[]{:S(2)}) %collective-permute-start.42) | collective-permute-done | bytes 672 | tf_op jit(solution)/shard_map/ppermute | solution.py:25
  658.2 12.4 collective-permute-done.43
  737.7 14.1 collective-permute-done.53
  753.7 12.9 collective-permute-done.54
  803.3 12.5 collective-permute-done.33
  827.6 12.0 collective-permute-done.37
  846.7 21.6 %collective-permute-start.57 = (f32[160,16]{0,1:T(8,128)S(1)}, f32[160,16]{0,1:T(8,128)S(1)}, u32[]{:S(2)}, u32[]{:S(2)}) collective-permute-start(f32[160,16]{0,1:T(8,128)S(1)} %bitcast.179), channel_id=1, source_target_pairs={{0,6},{1,7},{2,8},{3,9},{4,10},{5,11},{6,12},{7,13},{8,14},{9,15},... | collective-permute-start | bytes 30728 | tf_op jit(solution)/shard_map/ppermute | solution.py:25
  868.3 29.4 %collective-permute-done.39 = bf16[160,1024]{0,1:T(8,128)(2,1)} collective-permute-done((bf16[160,1024]{0,1:T(8,128)(2,1)}, bf16[160,1024]{0,1:T(8,128)(2,1)}, u32[]{:S(2)}, u32[]{:S(2)}) %collective-permute-start.39) | collective-permute-done | bytes 327712 | tf_op jit(solution)/shard_map/ppermute | solution.py:25
  897.7 12.4 collective-permute-start.58
  918.3 29.7 %collective-permute-done.41 = bf16[160,1024]{0,1:T(8,128)(2,1)} collective-permute-done((bf16[160,1024]{0,1:T(8,128)(2,1)}, bf16[160,1024]{0,1:T(8,128)(2,1)}, u32[]{:S(2)}, u32[]{:S(2)}) %collective-permute-start.41) | collective-permute-done | bytes 327712 | tf_op jit(solution)/shard_map/ppermute | solution.py:25
  955.5 19.8 %collective-permute-start.61 = (f32[160,16]{0,1:T(8,128)S(1)}, f32[160,16]{0,1:T(8,128)S(1)}, u32[]{:S(2)}, u32[]{:S(2)}) collective-permute-start(f32[160,16]{0,1:T(8,128)S(1)} %bitcast.183), channel_id=1, source_target_pairs={{0,2},{1,3},{2,4},{3,5},{4,6},{5,7},{6,8},{7,9},{8,10},{9,11},{10,... | collective-permute-start | bytes 30728 | tf_op jit(solution)/shard_map/ppermute | solution.py:25
  1075.3 92.2 %while.38 = (s32[]{:T(128)}, bf16[8,160,128]{1,2,0:T(8,128)(2,1)}, s32[8]{0:T(128)S(1)}, bf16[2400,1024]{0,1:T(8,128)(2,1)}, bf16[160,1024]{0,1:T(8,128)(2,1)}, ...) while((s32[]{:T(128)}, bf16[8,160,128]{1,2,0:T(8,128)(2,1)}, ...), condition=%wide.region_9.10_spmd.clone, body=%wide.region_8.9_spmd.clone.sunk | while | flops 300712960 | bytes 11706793 | solution.py:154
  1198.2 21.0 %collective-permute-done.97 = f32[160,16]{1,0:T(8,128)S(1)} collective-permute-done((f32[160,16]{1,0:T(8,128)}, f32[160,16]{1,0:T(8,128)S(1)}, u32[]{:S(2)}, u32[]{:S(2)}) %collective-permute-start.97) | collective-permute-done | bytes 10272 | tf_op jit(solution)/shard_map/ppermute | solution.py:25
  1278.5 17.6 %collective-permute-done.81 = bf16[160,1024]{1,0:T(8,128)(2,1)S(1)} collective-permute-done((bf16[160,1024]{1,0:T(8,128)(2,1)}, bf16[160,1024]{1,0:T(8,128)(2,1)S(1)}, u32[]{:S(2)}, u32[]{:S(2)}) %collective-permute-start.81) | collective-permute-done | bytes 327712 | tf_op jit(solution)/shard_map/ppermute | solution.py:25
  1296.1 18.1 %collective-permute-done.82 = bf16[160,1024]{1,0:T(8,128)(2,1)S(1)} collective-permute-done((bf16[160,1024]{1,0:T(8,128)(2,1)}, bf16[160,1024]{1,0:T(8,128)(2,1)S(1)}, u32[]{:S(2)}, u32[]{:S(2)}) %collective-permute-start.82) | collective-permute-done | bytes 327712 | tf_op jit(solution)/shard_map/ppermute | solution.py:25
  1314.2 17.3 %collective-permute-done.83 = bf16[160,1024]{1,0:T(8,128)(2,1)S(1)} collective-permute-done((bf16[160,1024]{1,0:T(8,128)(2,1)}, bf16[160,1024]{1,0:T(8,128)(2,1)S(1)}, u32[]{:S(2)}, u32[]{:S(2)}) %collective-permute-start.83) | collective-permute-done | bytes 327712 | tf_op jit(solution)/shard_map/ppermute | solution.py:25
  1334.2 141.4 %while.39 = (s32[]{:T(128)}, bf16[8,160,128]{1,2,0:T(8,128)(2,1)}, bf16[8,160,128]{1,2,0:T(8,128)(2,1)}, s32[8]{0:T(128)S(1)}, bf16[2400,1024]{0,1:T(8,128)(2,1)...) while((s32[]{:T(128)}, bf16[8,160,128]{1,2,0:T(8,128)(2,1)}, ...), condition=%wide.region_11.12_spmd.clone, body=%wide.region_10.11_spmd.clone.sunk | while | flops 400189440 | bytes 16806428 | solution.py:197
  (601 shorter events, 781.4 us)
Async XLA Ops:
  7.2 970.4 %all-gather.2.cloned.1.call-start = ((), (), s32[]{:S(2)}) async-start(), calls=%async_computation | async-start | bytes 2105344 | tf_op jit(solution)/shard_map/all_gather | solution.py:93
  22.2 81.5 %collective-permute-start.2 = (bf16[160,1024]{0,1:T(8,128)(2,1)}, bf16[160,1024]{0,1:T(8,128)(2,1)S(1)}, u32[]{:S(2)}, u32[]{:S(2)}) collective-permute-start(bf16[160,1024]{0,1:T(8,128)(2,1)} %copy.233), channel_id=1, source_target_pairs={{0,5},{1,6},{2,7},{3,8},{4,9},{5,10},{6,11},{7,12},{8,13},{9,14},{... | collective-permute-start | bytes 983048 | tf_op jit(solution)/shard_map/ppermute | solution.py:25
  24.1 92.3 %collective-permute-start.3 = (bf16[160,1024]{0,1:T(8,128)(2,1)}, bf16[160,1024]{0,1:T(8,128)(2,1)S(1)}, u32[]{:S(2)}, u32[]{:S(2)}) collective-permute-start(bf16[160,1024]{0,1:T(8,128)(2,1)} %copy.233), channel_id=1, source_target_pairs={{0,4},{1,5},{2,6},{3,7},{4,8},{5,9},{6,10},{7,11},{8,12},{9,13},{1... | collective-permute-start | bytes 983048 | tf_op jit(solution)/shard_map/ppermute | solution.py:25
  28.0 124.5 %collective-permute-start.4 = (bf16[160,1024]{0,1:T(8,128)(2,1)}, bf16[160,1024]{0,1:T(8,128)(2,1)S(1)}, u32[]{:S(2)}, u32[]{:S(2)}) collective-permute-start(bf16[160,1024]{0,1:T(8,128)(2,1)} %copy.233), channel_id=1, source_target_pairs={{0,3},{1,4},{2,5},{3,6},{4,7},{5,8},{6,9},{7,10},{8,11},{9,12},{10... | collective-permute-start | bytes 983048 | tf_op jit(solution)/shard_map/ppermute | solution.py:25
  65.1 92.2 %collective-permute-start.5 = (bf16[160,1024]{0,1:T(8,128)(2,1)}, bf16[160,1024]{0,1:T(8,128)(2,1)}, u32[]{:S(2)}, u32[]{:S(2)}) collective-permute-start(bf16[160,1024]{0,1:T(8,128)(2,1)} %copy.233), channel_id=1, source_target_pairs={{0,2},{1,3},{2,4},{3,5},{4,6},{5,7},{6,8},{7,9},{8,10},{9,11},{10,... | collective-permute-start | bytes 983048 | tf_op jit(solution)/shard_map/ppermute | solution.py:25
  81.0 82.0 %collective-permute-start.6 = (bf16[160,1024]{0,1:T(8,128)(2,1)}, bf16[160,1024]{0,1:T(8,128)(2,1)}, u32[]{:S(2)}, u32[]{:S(2)}) collective-permute-start(bf16[160,1024]{0,1:T(8,128)(2,1)} %copy.233), channel_id=1, source_target_pairs={{0,1},{1,2},{2,3},{3,4},{4,5},{5,6},{6,7},{7,8},{8,9},{9,10},{10,1... | collective-permute-start | bytes 983048 | tf_op jit(solution)/shard_map/ppermute | solution.py:25
  172.7 94.4 %collective-permute-start.12 = (bf16[160,1024]{0,1:T(8,128)(2,1)}, bf16[160,1024]{0,1:T(8,128)(2,1)}, u32[]{:S(2)}, u32[]{:S(2)}) collective-permute-start(bf16[160,1024]{0,1:T(8,128)(2,1)} %copy.233), channel_id=1, source_target_pairs={{6,0},{7,1},{8,2},{9,3},{10,4},{11,5},{12,6},{13,7},{14,8},{15,9},... | collective-permute-start | bytes 983048 | tf_op jit(solution)/shard_map/ppermute | solution.py:25
  175.0 878.5 %all-reduce.4.cloned.1.call-start = ((), (), s32[]{:S(2)}) async-start(), calls=%async_computation.1 | async-start | bytes 8388608
  180.2 120.0 %collective-permute-start.13 = (bf16[160,1024]{0,1:T(8,128)(2,1)}, bf16[160,1024]{0,1:T(8,128)(2,1)S(1)}, u32[]{:S(2)}, u32[]{:S(2)}) collective-permute-start(bf16[160,1024]{0,1:T(8,128)(2,1)} %copy.233), channel_id=1, source_target_pairs={{7,0},{8,1},{9,2},{10,3},{11,4},{12,5},{13,6},{14,7},{15,8},{16,9}... | collective-permute-start | bytes 983048 | tf_op jit(solution)/shard_map/ppermute | solution.py:25
  194.0 108.1 %collective-permute-start.14 = (bf16[160,1024]{0,1:T(8,128)(2,1)}, bf16[160,1024]{0,1:T(8,128)(2,1)S(1)}, u32[]{:S(2)}, u32[]{:S(2)}) collective-permute-start(bf16[160,1024]{0,1:T(8,128)(2,1)} %copy.248), channel_id=1, source_target_pairs={{0,7},{1,8},{2,9},{3,10},{4,11},{5,12},{6,13},{7,14},{8,15},{9,16}... | collective-permute-start | bytes 983048 | tf_op jit(solution)/shard_map/ppermute | solution.py:25
  205.3 106.6 %collective-permute-start.15 = (bf16[160,1024]{0,1:T(8,128)(2,1)}, bf16[160,1024]{0,1:T(8,128)(2,1)S(1)}, u32[]{:S(2)}, u32[]{:S(2)}) collective-permute-start(bf16[160,1024]{0,1:T(8,128)(2,1)} %copy.248), channel_id=1, source_target_pairs={{0,6},{1,7},{2,8},{3,9},{4,10},{5,11},{6,12},{7,13},{8,14},{9,15},... | collective-permute-start | bytes 983048 | tf_op jit(solution)/shard_map/ppermute | solution.py:25
  231.6 82.3 %collective-permute-start.16 = (bf16[160,1024]{0,1:T(8,128)(2,1)}, bf16[160,1024]{0,1:T(8,128)(2,1)S(1)}, u32[]{:S(2)}, u32[]{:S(2)}) collective-permute-start(bf16[160,1024]{0,1:T(8,128)(2,1)} %copy.248), channel_id=1, source_target_pairs={{0,5},{1,6},{2,7},{3,8},{4,9},{5,10},{6,11},{7,12},{8,13},{9,14},{... | collective-permute-start | bytes 983048 | tf_op jit(solution)/shard_map/ppermute | solution.py:25
  360.7 77.8 %collective-permute-start.26 = (bf16[160,1024]{0,1:T(8,128)(2,1)}, bf16[160,1024]{0,1:T(8,128)(2,1)}, u32[]{:S(2)}, u32[]{:S(2)}) collective-permute-start(bf16[160,1024]{0,1:T(8,128)(2,1)} %copy.248), channel_id=1, source_target_pairs={{6,0},{7,1},{8,2},{9,3},{10,4},{11,5},{12,6},{13,7},{14,8},{15,9},... | collective-permute-start | bytes 983048 | tf_op jit(solution)/shard_map/ppermute | solution.py:25
  365.0 93.6 %collective-permute-start.27 = (bf16[160,1024]{0,1:T(8,128)(2,1)}, bf16[160,1024]{0,1:T(8,128)(2,1)}, u32[]{:S(2)}, u32[]{:S(2)}) collective-permute-start(bf16[160,1024]{0,1:T(8,128)(2,1)} %copy.248), channel_id=1, source_target_pairs={{7,0},{8,1},{9,2},{10,3},{11,4},{12,5},{13,6},{14,7},{15,8},{16,9}... | collective-permute-start | bytes 983048 | tf_op jit(solution)/shard_map/ppermute | solution.py:25
  522.2 263.9 %collective-permute-start.28 = (bf16[160,1024]{0,1:T(8,128)(2,1)}, bf16[160,1024]{0,1:T(8,128)(2,1)S(1)}, u32[]{:S(2)}, u32[]{:S(2)}) collective-permute-start(bf16[160,1024]{0,1:T(8,128)(2,1)} %copy.263), channel_id=1, source_target_pairs={{0,7},{1,8},{2,9},{3,10},{4,11},{5,12},{6,13},{7,14},{8,15},{9,16}... | collective-permute-start | bytes 983048 | tf_op jit(solution)/shard_map/ppermute | solution.py:25
  536.7 252.7 %collective-permute-start.29 = (bf16[160,1024]{0,1:T(8,128)(2,1)}, bf16[160,1024]{0,1:T(8,128)(2,1)S(1)}, u32[]{:S(2)}, u32[]{:S(2)}) collective-permute-start(bf16[160,1024]{0,1:T(8,128)(2,1)} %copy.263), channel_id=1, source_target_pairs={{0,6},{1,7},{2,8},{3,9},{4,10},{5,11},{6,12},{7,13},{8,14},{9,15},... | collective-permute-start | bytes 983048 | tf_op jit(solution)/shard_map/ppermute | solution.py:25
  538.6 254.1 %collective-permute-start.30 = (bf16[160,1024]{0,1:T(8,128)(2,1)}, bf16[160,1024]{0,1:T(8,128)(2,1)S(1)}, u32[]{:S(2)}, u32[]{:S(2)}) collective-permute-start(bf16[160,1024]{0,1:T(8,128)(2,1)} %copy.263), channel_id=1, source_target_pairs={{0,5},{1,6},{2,7},{3,8},{4,9},{5,10},{6,11},{7,12},{8,13},{9,14},{... | collective-permute-start | bytes 983048 | tf_op jit(solution)/shard_map/ppermute | solution.py:25
  551.4 243.3 %collective-permute-start.31 = (bf16[160,1024]{0,1:T(8,128)(2,1)}, bf16[160,1024]{0,1:T(8,128)(2,1)S(1)}, u32[]{:S(2)}, u32[]{:S(2)}) collective-permute-start(bf16[160,1024]{0,1:T(8,128)(2,1)} %copy.263), channel_id=1, source_target_pairs={{0,4},{1,5},{2,6},{3,7},{4,8},{5,9},{6,10},{7,11},{8,12},{9,13},{1... | collective-permute-start | bytes 983048 | tf_op jit(solution)/shard_map/ppermute | solution.py:25
  554.5 99.1 %collective-permute-start.42 = (f32[160]{0:T(256)S(1)}, f32[160]{0:T(256)S(1)}, u32[]{:S(2)}, u32[]{:S(2)}) collective-permute-start(f32[160]{0:T(256)S(1)} %get-tuple-element.493), channel_id=1, source_target_pairs={{0,7},{1,8},{2,9},{3,10},{4,11},{5,12},{6,13},{7,14},{8,15},{9,16}... | collective-permute-start | bytes 1928 | tf_op jit(solution)/shard_map/ppermute | solution.py:25
  821.8 75.9 %collective-permute-start.39 = (bf16[160,1024]{0,1:T(8,128)(2,1)}, bf16[160,1024]{0,1:T(8,128)(2,1)}, u32[]{:S(2)}, u32[]{:S(2)}) collective-permute-start(bf16[160,1024]{0,1:T(8,128)(2,1)} %copy.263), channel_id=1, source_target_pairs={{5,0},{6,1},{7,2},{8,3},{9,4},{10,5},{11,6},{12,7},{13,8},{14,9},{... | collective-permute-start | bytes 983048 | tf_op jit(solution)/shard_map/ppermute | solution.py:25
  823.7 86.4 %collective-permute-start.40 = (bf16[160,1024]{0,1:T(8,128)(2,1)}, bf16[160,1024]{0,1:T(8,128)(2,1)}, u32[]{:S(2)}, u32[]{:S(2)}) collective-permute-start(bf16[160,1024]{0,1:T(8,128)(2,1)} %copy.263), channel_id=1, source_target_pairs={{6,0},{7,1},{8,2},{9,3},{10,4},{11,5},{12,6},{13,7},{14,8},{15,9},... | collective-permute-start | bytes 983048 | tf_op jit(solution)/shard_map/ppermute | solution.py:25
  825.7 122.3 %collective-permute-start.41 = (bf16[160,1024]{0,1:T(8,128)(2,1)}, bf16[160,1024]{0,1:T(8,128)(2,1)}, u32[]{:S(2)}, u32[]{:S(2)}) collective-permute-start(bf16[160,1024]{0,1:T(8,128)(2,1)} %copy.263), channel_id=1, source_target_pairs={{7,0},{8,1},{9,2},{10,3},{11,4},{12,5},{13,6},{14,7},{15,8},{16,9}... | collective-permute-start | bytes 983048 | tf_op jit(solution)/shard_map/ppermute | solution.py:25
  839.7 115.8 %collective-permute-start.56 = (f32[160,16]{0,1:T(8,128)S(1)}, f32[160,16]{0,1:T(8,128)S(1)}, u32[]{:S(2)}, u32[]{:S(2)}) collective-permute-start(f32[160,16]{0,1:T(8,128)S(1)} %bitcast.178), channel_id=1, source_target_pairs={{0,7},{1,8},{2,9},{3,10},{4,11},{5,12},{6,13},{7,14},{8,15},{9,16}... | collective-permute-start | bytes 30728 | tf_op jit(solution)/shard_map/ppermute | solution.py:25
  846.7 128.7 %collective-permute-start.57 = (f32[160,16]{0,1:T(8,128)S(1)}, f32[160,16]{0,1:T(8,128)S(1)}, u32[]{:S(2)}, u32[]{:S(2)}) collective-permute-start(f32[160,16]{0,1:T(8,128)S(1)} %bitcast.179), channel_id=1, source_target_pairs={{0,6},{1,7},{2,8},{3,9},{4,10},{5,11},{6,12},{7,13},{8,14},{9,15},... | collective-permute-start | bytes 30728 | tf_op jit(solution)/shard_map/ppermute | solution.py:25
  897.7 82.7 %collective-permute-start.58 = (f32[160,16]{0,1:T(8,128)S(1)}, f32[160,16]{0,1:T(8,128)S(1)}, u32[]{:S(2)}, u32[]{:S(2)}) collective-permute-start(f32[160,16]{0,1:T(8,128)S(1)} %bitcast.180), channel_id=1, source_target_pairs={{0,5},{1,6},{2,7},{3,8},{4,9},{5,10},{6,11},{7,12},{8,13},{9,14},{... | collective-permute-start | bytes 30728 | tf_op jit(solution)/shard_map/ppermute | solution.py:25
  910.2 72.7 %collective-permute-start.59 = (f32[160,16]{0,1:T(8,128)S(1)}, f32[160,16]{0,1:T(8,128)S(1)}, u32[]{:S(2)}, u32[]{:S(2)}) collective-permute-start(f32[160,16]{0,1:T(8,128)S(1)} %bitcast.181), channel_id=1, source_target_pairs={{0,4},{1,5},{2,6},{3,7},{4,8},{5,9},{6,10},{7,11},{8,12},{9,13},{1... | collective-permute-start | bytes 30728 | tf_op jit(solution)/shard_map/ppermute | solution.py:25
  1055.8 111.8 %collective-permute-start.92 = (f32[160,16]{1,0:T(8,128)}, f32[160,16]{1,0:T(8,128)}, u32[]{:S(2)}, u32[]{:S(2)}) collective-permute-start(f32[160,16]{1,0:T(8,128)} %reduce_sum.28), channel_id=1, source_target_pairs={{2,0},{3,1},{4,2},{5,3},{6,4},{7,5},{8,6},{9,7},{10,8},{11,9},{12,... | collective-permute-start | bytes 30728 | tf_op jit(solution)/shard_map/ppermute | solution.py:25
  1059.9 113.0 %collective-permute-start.93 = (f32[160,16]{1,0:T(8,128)}, f32[160,16]{1,0:T(8,128)}, u32[]{:S(2)}, u32[]{:S(2)}) collective-permute-start(f32[160,16]{1,0:T(8,128)} %reduce_sum.28), channel_id=1, source_target_pairs={{3,0},{4,1},{5,2},{6,3},{7,4},{8,5},{9,6},{10,7},{11,8},{12,9},{13... | collective-permute-start | bytes 30728 | tf_op jit(solution)/shard_map/ppermute | solution.py:25
  1062.4 116.9 %collective-permute-start.94 = (f32[160,16]{1,0:T(8,128)}, f32[160,16]{1,0:T(8,128)}, u32[]{:S(2)}, u32[]{:S(2)}) collective-permute-start(f32[160,16]{1,0:T(8,128)} %reduce_sum.28), channel_id=1, source_target_pairs={{4,0},{5,1},{6,2},{7,3},{8,4},{9,5},{10,6},{11,7},{12,8},{13,9},{1... | collective-permute-start | bytes 30728 | tf_op jit(solution)/shard_map/ppermute | solution.py:25
  1064.7 116.6 %collective-permute-start.95 = (f32[160,16]{1,0:T(8,128)}, f32[160,16]{1,0:T(8,128)}, u32[]{:S(2)}, u32[]{:S(2)}) collective-permute-start(f32[160,16]{1,0:T(8,128)} %reduce_sum.28), channel_id=1, source_target_pairs={{5,0},{6,1},{7,2},{8,3},{9,4},{10,5},{11,6},{12,7},{13,8},{14,9},{... | collective-permute-start | bytes 30728 | tf_op jit(solution)/shard_map/ppermute | solution.py:25
  1066.8 155.3 %collective-permute-start.70 = (bf16[160,1024]{1,0:T(8,128)(2,1)}, bf16[160,1024]{1,0:T(8,128)(2,1)}, u32[]{:S(2)}, u32[]{:S(2)}) collective-permute-start(bf16[160,1024]{1,0:T(8,128)(2,1)} %get-tuple-element.804), channel_id=1, source_target_pairs={{0,7},{1,8},{2,9},{3,10},{4,11},{5,12},{6,13},{7,14},{8,15},{9,16}... | collective-permute-start | bytes 983048 | tf_op jit(solution)/shard_map/ppermute | solution.py:25
  1255.7 75.9 %collective-permute-start.83 = (bf16[160,1024]{1,0:T(8,128)(2,1)}, bf16[160,1024]{1,0:T(8,128)(2,1)S(1)}, u32[]{:S(2)}, u32[]{:S(2)}) collective-permute-start(bf16[160,1024]{1,0:T(8,128)(2,1)} %get-tuple-element.804), channel_id=1, source_target_pairs={{7,0},{8,1},{9,2},{10,3},{11,4},{12,5},{13,6},{14,7},{15,8},{16,9}... | collective-permute-start | bytes 983048 | tf_op jit(solution)/shard_map/ppermute | solution.py:25
  (121 other events, 6424.4 us)
Sparse Core Ops, SparseCore 0:
  175.1 183.8 all-gather.1
  522.3 454.7 all-reduce.3
where the time goes:
time: 1500 us; the launch traced here: 1490 us
  waiting for transfers between devices  652 us (43%)
  starting transfers between devices  460 us (31%)
  local copies, waits for them, and re-layouts  210 us (14%)
  matrix products  103 us (7%)
  loops' own time  27.1 us (2%)
  other arithmetic  19.3 us (1%)
  between operations  16 us (1%)
    ppermute x98, waiting for transfers between devices, passed_along(): return lax.ppermute(block, axis, route)  652 us
    ppermute x98, starting transfers between devices, passed_along(): return lax.ppermute(block, axis, route)  459 us
    dynamic_slice x80, local copies, waits for them, and re-layouts, column_slice(): lax.dynamic_slice_in_dim(block, group_index * group_cols, group_cols, 1)  107 us
    concatenate x7, local copies, waits for them, and re-layouts, join_rows(): return jax.tree.map(lambda *blocks: jnp.concatenate(blocks, 0), *pieces)  34 us
  transfers between devices with their start and end apart: 100, of which 46 were waited for; matrix products, arithmetic and copies ran while one was open for 13% of the time, Pallas kernels for 0%

commit v1 on v0

v1 whole, which is shorter than its diff:
```python
import functools
import math

import jax
import jax.numpy as jnp
from jax import lax
from jax.experimental import pallas as pl
from jax.experimental.pallas import tpu as pltpu
from jax.sharding import PartitionSpec as P

D = 1024
HEADS = 16
HEAD = 64
WIN = 1120
RIM = 1120
TQ = 128
SPAN = 2432
FAR = -1e30
MESH = pl.DeviceIdType.MESH
BF16 = jnp.bfloat16
F32 = jnp.float32
VMEM_LIMIT = 56 * 1024 * 1024


def spot():
    me = lax.axis_index("seq")
    return me, me // HEADS, lax.rem(me, HEADS)


def push(src, dst, send, recv, device):
    return pltpu.make_async_remote_copy(
        src_ref=src, dst_ref=dst, send_sem=send, recv_sem=recv, device_id=(device,), device_id_type=MESH
    )


def meet(devices):
    barrier = pltpu.get_barrier_semaphore()
    for device in devices:
        pl.semaphore_signal(barrier, inc=1, device_id=(device,), device_id_type=MESH)
    pl.semaphore_wait(barrier, len(devices))


def lanes_low(shape):
    return lax.broadcasted_iota(jnp.int32, shape, 1) < HEAD


def pair_up(left, right, out, points):
    for k in range(HEADS // 2):
        cols = pl.ds(2 * HEAD * k, 2 * HEAD)
        a, b = left[:, cols], right[:, cols]
        out[2 * k] = jnp.concatenate([a[:, :HEAD], b[:, :HEAD]], axis=1)
        out[2 * k + 1] = jnp.concatenate([a[:, HEAD:], b[:, HEAD:]], axis=1)


def split_up(blocks, left, right):
    for k in range(HEADS // 2):
        cols = pl.ds(2 * HEAD * k, 2 * HEAD)
        a, b = blocks[2 * k], blocks[2 * k + 1]
        left[:, cols] = jnp.concatenate([a[:, :HEAD], b[:, :HEAD]], axis=1)
        right[:, cols] = jnp.concatenate([a[:, HEAD:], b[:, HEAD:]], axis=1)


def gather_kernel(
    rows,
    q_ref, k_ref, v_ref, cot_ref, w_ref, st_ref,
    kv_ref, qg_ref, starts_ref, weight_ref,
    kv_send, qg_send, st_recv, w_recv, w_wide, grad,
    kv_ss, kv_rs, qg_ss, qg_rs, st_ss, st_rs, w_ss, w_rs, x_ss, x_rs, s_ss, s_rs, rim_ss, rim_rs,
):
    me, row, place = spot()
    core = lax.rem(me, 2)
    points = q_ref.shape[0]
    span = HEADS * points
    sibling = me + 1 - 2 * core
    mates = [row * HEADS + lax.rem(place + i, HEADS) for i in range(1, HEADS)]
    peers = [lax.rem(row + i, rows) * HEADS + place for i in range(1, rows)]
    lower = lax.rem(row + rows - 1, rows) * HEADS + place
    upper = lax.rem(row + 1, rows) * HEADS + place
    meet(mates + peers)

    live = []

    def go(copy):
        copy.start()
        live.append(copy)
        return copy

    part = w_ref.shape[0]
    w_copies = [
        go(push(w_ref, w_recv.at[pl.ds(place * part, part)], w_ss.at[i], w_rs.at[i], mates[i]))
        for i in range(HEADS - 1)
    ]
    w_recv[pl.ds(pl.multiple_of(place * part, part), part)] = w_ref[...]
    st_copies = [
        go(push(st_ref, st_recv.at[place], st_ss.at[i], st_rs.at[i], mates[i])) for i in range(HEADS - 1)
    ]
    st_recv[place] = st_ref[...]

    pair_up(k_ref, v_ref, kv_send, points)
    mine = pl.ds(pl.multiple_of(RIM + place * points, 16), points)
    kv_copies = [
        go(push(kv_send.at[lax.rem(place + i + 1, HEADS)], kv_ref.at[mine], kv_ss.at[i], kv_rs.at[i], mates[i]))
        for i in range(HEADS - 1)
    ]
    kv_ref[mine] = kv_send[place]
    tail = kv_ref.shape[0] - (2 * RIM + span)
    kv_ref[pl.ds(2 * RIM + span, tail)] = jnp.zeros((tail, 2 * HEAD), BF16)

    for copy in w_copies:
        copy.wait_recv()
    w_wide[...] = w_recv[...].astype(F32)
    wrows = HEADS * part * 2 * HEAD // D
    half = wrows // 2
    own = pl.multiple_of(row * wrows, 16)
    for b in range(D // 128):
        weight_ref[pl.ds(own, wrows), pl.ds(b * 128, 128)] = w_wide[pl.ds(b, wrows, stride=D // 128), :].astype(BF16)
    my_half = weight_ref.at[pl.ds(pl.multiple_of(own + core * half, 16), half)]
    x_copies = [go(push(my_half, my_half, x_ss.at[i], x_rs.at[i], peers[i])) for i in range(rows - 1)]

    for copy in kv_copies:
        copy.wait_recv()
    rim_copies = [
        go(push(kv_ref.at[pl.ds(RIM, RIM)], kv_ref.at[pl.ds(RIM + span, RIM)], rim_ss.at[0], rim_rs.at[0], lower)),
        go(push(kv_ref.at[pl.ds(span, RIM)], kv_ref.at[pl.ds(0, RIM)], rim_ss.at[1], rim_rs.at[1], upper)),
    ]

    s_copies = []
    for i in range(rows - 1):
        x_copies[i].wait_recv()
        source = lax.rem(row + rows - i - 1, rows)
        came = weight_ref.at[pl.ds(pl.multiple_of(source * wrows + core * half, 16), half)]
        s_copies.append(go(push(came, came, s_ss.at[i], s_rs.at[i], sibling)))
    for copy in s_copies:
        copy.wait_recv()

    grad[...] = lax.dot_general(
        cot_ref[...], weight_ref[...], (((1,), (1,)), ((), ())), preferred_element_type=F32
    ).astype(BF16)
    pair_up(q_ref, grad, qg_send, points)
    here = pl.ds(pl.multiple_of(place * points, 16), points)
    qg_copies = [
        go(push(qg_send.at[lax.rem(place + i + 1, HEADS)], qg_ref.at[here], qg_ss.at[i], qg_rs.at[i], mates[i]))
        for i in range(HEADS - 1)
    ]
    qg_ref[here] = qg_send[place]

    for copy in st_copies:
        copy.wait_recv()
    for t in range(span // TQ):
        total = None
        for p in range(HEADS):
            first = p * points // TQ
            if first <= t <= first + 1:
                piece = st_recv[p, 0:1, pl.ds((t - first) * TQ, TQ)]
                total = piece if total is None else total + piece
        starts_ref[t : t + 1, :] = total

    for copy in rim_copies:
        copy.wait_recv()
    for copy in qg_copies:
        copy.wait_recv()
    for copy in live:
        copy.wait_send()


def attend_kernel(kv_ref, qg_ref, starts_ref, base_ref, oq_ref, dkv_ref, kvt, acc, scores, slants, pairs):
    low = lanes_low((TQ, 2 * HEAD))
    scale = 1.0 / math.sqrt(HEAD)
    fold = scale * math.log2(math.e)
    chunks = [(k, min(256, SPAN - k)) for k in range(0, SPAN, 256)]

    @pl.loop(0, kv_ref.shape[0] // 128)
    def _(t):
        at = pl.ds(pl.multiple_of(t * 128, 128), 128)
        kvt[:, at] = kv_ref[at, :].astype(F32).T.astype(BF16)
        acc[at, :] = jnp.zeros((128, 2 * HEAD), F32)

    @pl.loop(0, qg_ref.shape[0] // TQ)
    def _(t):
        first = pl.multiple_of(t * TQ, TQ)
        qg = qg_ref[pl.ds(first, TQ), :]
        zero = jnp.zeros_like(qg)
        both = jnp.concatenate([jnp.where(low, qg, zero), jnp.where(low, zero, qg)], axis=0)
        rel = starts_ref[pl.ds(t, 1), :] - base_ref[0] - first
        top = jnp.full((8, TQ), FAR, F32)
        for k, n in chunks:
            made = lax.dot_general(
                kv_ref[pl.ds(first + k, n), :], both, (((1,), (1,)), ((), ())), preferred_element_type=F32
            )
            past = lax.broadcasted_iota(jnp.int32, (n, TQ), 0) - (rel - k)
            s = jnp.where((past >= 0) & (past < WIN), made[:, :TQ] * fold, FAR)
            scores[pl.ds(k, n), :] = s
            slants[pl.ds(k, n), :] = made[:, TQ:]
            top = jnp.maximum(top, jnp.max(s.reshape(n // 8, 8, TQ), axis=0))
        top = jnp.max(top, axis=0, keepdims=True)
        total = jnp.zeros((8, TQ), F32)
        cross = jnp.zeros((8, TQ), F32)
        out_t = jnp.zeros((HEAD, TQ), F32)
        for k, n in chunks:
            p = jnp.exp2(scores[pl.ds(k, n), :] - top)
            total += jnp.sum(p.reshape(n // 8, 8, TQ), axis=0)
            cross += jnp.sum((p * slants[pl.ds(k, n), :]).reshape(n // 8, 8, TQ), axis=0)
            p = p.astype(BF16)
            pairs[pl.ds(k, n), TQ:] = p
            out_t += jnp.dot(kvt[HEAD:, pl.ds(first + k, n)], p, preferred_element_type=F32)
        share = 1.0 / jnp.sum(total, axis=0, keepdims=True)
        delta = jnp.sum(cross, axis=0, keepdims=True) * share
        by_row = jnp.broadcast_to(share, (TQ, TQ)).T
        scaled = qg.astype(F32) * by_row
        scaled = jnp.concatenate(
            [jnp.where(low, scaled * scale, 0.0), jnp.where(low, 0.0, scaled)], axis=0
        ).astype(BF16)
        dq_t = jnp.zeros((HEAD, TQ), F32)
        for k, n in chunks:
            p = pairs[pl.ds(k, n), TQ:].astype(F32)
            ds = (p * (slants[pl.ds(k, n), :] - delta)).astype(BF16)
            pairs[pl.ds(k, n), :TQ] = ds
            dq_t += jnp.dot(kvt[:HEAD, pl.ds(first + k, n)], ds, preferred_element_type=F32)
            acc[pl.ds(first + k, n), :] += jnp.dot(pairs[pl.ds(k, n), :], scaled, preferred_element_type=F32)
        back = jnp.concatenate([dq_t * (share * scale), out_t * share], axis=0)
        oq_ref[pl.ds(first, TQ), :] = back.T.astype(BF16)

    @pl.loop(0, kv_ref.shape[0] // 128)
    def _(t):
        at = pl.ds(pl.multiple_of(t * 128, 128), 128)
        dkv_ref[at, :] = acc[at, :].astype(BF16)


def scatter_kernel(
    rows, inverse_root,
    oq_ref, dkv_ref, cot_ref, weight_ref,
    out_ref, dq_ref, dk_ref, dv_ref, dw_ref,
    oq_recv, kv_recv, rim_recv, kv_sum, mixed, terms, sib_recv, half_sum, peer_recv, flat, last_recv,
    oq_ss, oq_rs, kv_ss, kv_rs, rim_ss, rim_rs, s_ss, s_rs, x_ss, x_rs, z_ss, z_rs,
):
    me, row, place = spot()
    core = lax.rem(me, 2)
    points = cot_ref.shape[0]
    span = HEADS * points
    sibling = me + 1 - 2 * core
    mates = [row * HEADS + lax.rem(place + i, HEADS) for i in range(1, HEADS)]
    peers = [lax.rem(row + i, rows) * HEADS + place for i in range(1, rows)]
    lower = lax.rem(row + rows - 1, rows) * HEADS + place
    upper = lax.rem(row + 1, rows) * HEADS + place
    meet(mates + peers)

    live = []

    def go(copy):
        copy.start()
        live.append(copy)
        return copy

    def block(at, offset=0):
        return pl.ds(pl.multiple_of(offset + at * points, 16), points)

    oq_copies = [
        go(push(oq_ref.at[block(lax.rem(place + i + 1, HEADS))], oq_recv.at[place], oq_ss.at[i], oq_rs.at[i], mates[i]))
        for i in range(HEADS - 1)
    ]
    oq_recv[place] = oq_ref[block(place), :]
    rim_copies = [
        go(push(dkv_ref.at[pl.ds(0, RIM)], rim_recv.at[1], rim_ss.at[0], rim_rs.at[0], lower)),
        go(push(dkv_ref.at[pl.ds(RIM + span, RIM)], rim_recv.at[0], rim_ss.at[1], rim_rs.at[1], upper)),
    ]
    for copy in rim_copies:
        copy.wait_recv()
    kv_sum[pl.ds(0, RIM), :] = (dkv_ref[pl.ds(RIM, RIM), :].astype(F32) + rim_recv[0].astype(F32)).astype(BF16)
    kv_sum[pl.ds(RIM, span - 2 * RIM), :] = dkv_ref[pl.ds(2 * RIM, span - 2 * RIM), :]
    kv_sum[pl.ds(span - RIM, RIM), :] = (dkv_ref[pl.ds(span, RIM), :].astype(F32) + rim_recv[1].astype(F32)).astype(BF16)
    kv_copies = [
        go(push(kv_sum.at[block(lax.rem(place + i + 1, HEADS))], kv_recv.at[place], kv_ss.at[i], kv_rs.at[i], mates[i]))
        for i in range(HEADS - 1)
    ]
    kv_recv[place] = kv_sum[block(place), :]

    for copy in oq_copies:
        copy.wait_recv()
    split_up(oq_recv, dq_ref, mixed)

    half = HEAD // 2
    for k in range(HEADS // 2):
        term = lax.dot_general(
            mixed[:, pl.ds(2 * HEAD * k, 2 * HEAD)], cot_ref[...], (((0,), (0,)), ((), ())), preferred_element_type=F32
        ).astype(BF16)
        for j in range(4):
            terms[j % 2, pl.ds((2 * k + j // 2) * half, half), :] = term[j * half : (j + 1) * half]
    s_copy = go(push(terms.at[1 - core], sib_recv, s_ss, s_rs, sibling))
    out_ref[...] = jnp.dot(mixed[...], weight_ref[...], preferred_element_type=F32).astype(BF16)
    s_copy.wait_recv()

    def to_sum(r):
        return pl.ds(pl.multiple_of(r * half, half), half)

    x_copies = []
    for i in list(range(1, rows)) + [0]:
        at = to_sum(lax.rem(row + i, rows))
        half_sum[at, :] = (terms[core, at, :].astype(F32) + sib_recv[at, :].astype(F32)).astype(BF16)
        if i:
            x_copies.append(
                go(push(half_sum.at[at], peer_recv.at[i - 1], x_ss.at[i - 1], x_rs.at[i - 1], peers[i - 1]))
            )
    total = half_sum[to_sum(row), :].astype(F32)
    for i in range(rows - 1):
        x_copies[i].wait_recv()
        total += peer_recv[i].astype(F32)
    total = total * inverse_root
    for b in range(D // 128):
        flat[pl.ds(b, half, stride=D // 128), :] = total[:, b * 128 : (b + 1) * 128]

    own = place // 2
    part = dw_ref.shape[0]
    z_copies = []
    for j in range(HEADS // 2):
        goal = core * (HEADS // 2) + j
        piece = flat.at[pl.ds(j * part, part)]
        copy = push(piece, last_recv.at[own], z_ss.at[j], z_rs.at[own], row * HEADS + goal)

        @pl.when(goal != place)
        def _():
            copy.start()

        @pl.when(goal == place)
        def _():
            last_recv[own] = flat[pl.ds(j * part, part), :]

        z_copies.append((goal, copy))

    for copy in kv_copies:
        copy.wait_recv()
    split_up(kv_recv, dk_ref, dv_ref)

    for z in range(HEADS // 2):
        source = 2 * z + place // (HEADS // 2)

        @pl.when(source != place)
        def _():
            push(flat.at[pl.ds(0, part)], last_recv.at[z], z_ss.at[0], z_rs.at[z], row * HEADS + source).wait_recv()

    dw_ref[...] = jnp.sum(last_recv[...], axis=0)
    for goal, copy in z_copies:

        @pl.when(goal != place)
        def _():
            copy.wait_send()

    for copy in live:
        copy.wait_send()


def window_starts(row_lengths, window_shift, first_point, all_points):
    count = row_lengths.shape[0]
    order = jnp.arange(count, dtype=jnp.int32)
    ends = jnp.sum(jnp.where(order[:, None] <= order[None, :], row_lengths[:, None], 0), axis=0)
    index = first_point + jnp.arange(window_shift.shape[0], dtype=jnp.int32)
    passed = ends[None, :] <= index[:, None]
    row_first = jnp.sum(jnp.where(passed, row_lengths[None, :], 0), axis=1)
    return jnp.clip(row_first - window_shift, 0, all_points - WIN)


def in_vmem(count):
    return [pl.BlockSpec(memory_space=pltpu.VMEM)] * count


def per_device(queries, key_rows, value_rows, out_weight, cotangent, row_lengths, window_shift):
    points = queries.shape[0]
    devices = lax.axis_size("seq")
    rows = devices // HEADS
    span = HEADS * points
    held = span - TQ + SPAN
    me = lax.axis_index("seq")
    starts = window_starts(row_lengths, window_shift, me * points, devices * points)
    offset = lax.rem(lax.rem(me, HEADS) * points, TQ)
    starts = lax.dynamic_update_slice(jnp.zeros((1, 2 * TQ), jnp.int32), starts[None, :], (0, offset))
    starts = jnp.concatenate([starts, jnp.zeros((7, 2 * TQ), jnp.int32)], axis=0)
    w_part = out_weight.shape[0] // 128
    wide = 2 * HEAD
    dma = pltpu.SemaphoreType.DMA
    ring, cross = dma((HEADS - 1,)), dma((rows - 1,))

    kv, qg, row_starts, weight = pl.pallas_call(
        functools.partial(gather_kernel, rows),
        out_shape=(
            jax.ShapeDtypeStruct((held, wide), BF16),
            jax.ShapeDtypeStruct((span, wide), BF16),
            jax.ShapeDtypeStruct((span // TQ, TQ), jnp.int32),
            jax.ShapeDtypeStruct((D, D), BF16),
        ),
        in_specs=in_vmem(6),
        out_specs=tuple(in_vmem(4)),
        scratch_shapes=[
            pltpu.VMEM((HEADS, points, wide), BF16),
            pltpu.VMEM((HEADS, points, wide), BF16),
            pltpu.VMEM((HEADS, 8, 2 * TQ), jnp.int32),
            pltpu.VMEM((HEADS * w_part, 128), BF16),
            pltpu.VMEM((HEADS * w_part, 128), F32),
            pltpu.VMEM((points, D), BF16),
            ring, ring, ring, ring, ring, ring, ring, ring, cross, cross, cross, cross, dma((2,)), dma((2,)),
        ],
        compiler_params=pltpu.CompilerParams(
            collective_id=0, has_side_effects=True, vmem_limit_bytes=VMEM_LIMIT
        ),
        name="gather_heads",
    )(queries, key_rows, value_rows, cotangent, out_weight.reshape(w_part, 128), starts)

    base = (me // HEADS * span - RIM).reshape(1)
    oq, dkv = pl.pallas_call(
        attend_kernel,
        out_shape=(jax.ShapeDtypeStruct((span, wide), BF16), jax.ShapeDtypeStruct((held, wide), BF16)),
        in_specs=in_vmem(3) + [pl.BlockSpec(memory_space=pltpu.SMEM)],
        out_specs=tuple(in_vmem(2)),
        scratch_shapes=[
            pltpu.VMEM((wide, held), BF16),
            pltpu.VMEM((held, wide), F32),
            pltpu.VMEM((SPAN, TQ), F32),
            pltpu.VMEM((SPAN, TQ), F32),
            pltpu.VMEM((SPAN, 2 * TQ), BF16),
        ],
        compiler_params=pltpu.CompilerParams(vmem_limit_bytes=VMEM_LIMIT),
        name="attend",
    )(kv, qg, row_starts, base)

    half = HEAD // 2
    full = jax.ShapeDtypeStruct((points, D), BF16)
    out, dq, dk, dv, dw = pl.pallas_call(
        functools.partial(scatter_kernel, rows, 1.0 / math.sqrt(devices * points)),
        out_shape=(full, full, full, full, jax.ShapeDtypeStruct((w_part, 128), F32)),
        in_specs=in_vmem(4),
        out_specs=tuple(in_vmem(5)),
        scratch_shapes=[
            pltpu.VMEM((HEADS, points, wide), BF16),
            pltpu.VMEM((HEADS, points, wide), BF16),
            pltpu.VMEM((2, RIM, wide), BF16),
            pltpu.VMEM((span, wide), BF16),
            pltpu.VMEM((points, D), BF16),
            pltpu.VMEM((2, HEADS * half, D), BF16),
            pltpu.VMEM((HEADS * half, D), BF16),
            pltpu.VMEM((HEADS * half, D), BF16),
            pltpu.VMEM((rows - 1, half, D), BF16),
            pltpu.VMEM((half * D // 128, 128), F32),
            pltpu.VMEM((HEADS // 2, w_part, 128), F32),
            ring, ring, ring, ring, dma((2,)), dma((2,)), dma, dma, cross, cross,
            dma((HEADS // 2,)), dma((HEADS // 2,)),
        ],
        compiler_params=pltpu.CompilerParams(
            collective_id=1, has_side_effects=True, vmem_limit_bytes=VMEM_LIMIT
        ),
        name="scatter_heads",
    )(oq, dkv, cotangent, weight)
    return (out, dq, dk, dv, dw.reshape(-1))


def solution(mesh):
    whole = P("seq", None)
    return jax.shard_map(
        per_device,
        mesh=mesh,
        in_specs=(whole, whole, whole, P("seq"), whole, P(), P("seq")),
        out_specs=(whole, whole, whole, whole, P("seq")),
        check_vma=False,
    )
```

time: 1500 us -> 162 us (0.11)
  waiting for transfers between devices: 652 us -> 0 us
  starting transfers between devices: 460 us -> 0 us
  local copies, waits for them, and re-layouts: 210 us -> 6.39 us
  Pallas kernels: 0 us -> 152 us
  matrix products: 103 us -> 0 us
  loops' own time: 27.1 us -> 0 us
  other arithmetic: 19.3 us -> 2.35 us
  between operations: 16 us -> 0.72 us
    ppermute x98 -> x0, waiting for transfers between devices: 652 us -> none  [passed_along(): return lax.ppermute(block, axis, route)]
    ppermute x98 -> x0, starting transfers between devices: 459 us -> none  [passed_along(): return lax.ppermute(block, axis, route)]
    pallas_call x0 -> x3, Pallas kernels: none -> 152 us  [the longest x1 60.6 us: per_device(): pl.pallas_call(functools.partial(gather_kernel, rows), out_shape=(jax.Sha...]
    dynamic_slice x104 -> x0, local copies, waits for them, and re-layouts: 121 us -> none  [the longest x80 107 us: column_slice(): lax.dynamic_slice_in_dim(block, group_index * group_cols, group_cols, 1)]
    dot_general x59 -> x0, matrix products: 103 us -> none  [the longest x8 18.8 us: query_group(): jnp.einsum('hqk,khd->qhd', slopes, key_part, preferred_element_type=jnp.f...]
    concatenate x7 -> x1, local copies, waits for them, and re-layouts: 34 us -> 0.61 us  [per_device(): jnp.concatenate([starts, jnp.zeros((7, 2 * TQ), jnp.int32)], axis=0)]
    another operation x3 -> x0, loops' own time: 27.1 us -> none  [the longest x1 10.8 us: per_device(): lax.map(query_group, group_list)]
  transfers between devices with their start and end apart: 100 -> 0, of which waited for: 46 -> 0; matrix products, arithmetic and copies ran while one was open for 13% -> 0% of each run, Pallas kernels for 0% -> 0%
where the time goes in v1:
time: 162 us
  Pallas kernels  152 us (94%)
  local copies, waits for them, and re-layouts  6.39 us (4%)
  other arithmetic  2.35 us (1%)
    pallas_call x1, Pallas kernels, per_device(): pl.pallas_call(functools.partial(gather_kernel, rows), out_shape=(jax.Sha...  60.6 us
    pallas_call x1, Pallas kernels, per_device(): pl.pallas_call(functools.partial(scatter_kernel, rows, 1.0 / math.sqrt(de...  49 us
    pallas_call x1, Pallas kernels, per_device(): pl.pallas_call(attend_kernel, out_shape=(jax.ShapeDtypeStruct((span, wide...  42.7 us
    unnamed x11, local copies, waits for them, and re-layouts  5.56 us

profile of v1, /device:TPU:25, one launch (start us, length us, event | category | flops | bytes accessed | tf_op | source)
XLA Modules:
  0.0 161.6 jit_solution(5551077551477454141)
XLA Ops:
  0.7 0.8 select_reduce_fusion
  1.5 0.9 select_reduce_fusion.1
  2.3 0.7 subtract_clamp_fusion
  3.0 0.2 dynamic_update_slice.3
  3.2 0.6 concatenate.3.st_ref
  3.9 60.6 %gather_heads.1 = (bf16[4864,128]{1,0:T(8,128)(2,1)}, bf16[2560,128]{1,0:T(8,128)(2,1)}, s32[20,128]{1,0:T(8,128)}, bf16[1024,1024]{1,0:T(8,128)(2,1)}) custom-call(bf16[160,1024]{1,0:T(8,128)(2,1)} %q_ref.1, bf16[160,1024]{1,0:T(8,128)(2,1)} %k_ref.1, bf16[160,1024]{1,0:T(8,128)(2,1)} %v_ref.1, bf16[160,1024]{1,0:T(8,128)(2,1)} %cot_ref.3, ...), custom_call_target="tpu_custom_call" | custom-call | tf_op jit(solution)/shard_map/gather_heads/pallas_call | solution.py:381
  64.4 42.7 %attend.1 = (bf16[2560,128]{1,0:T(8,128)(2,1)}, bf16[4864,128]{1,0:T(8,128)(2,1)}) custom-call(bf16[4864,128]{1,0:T(8,128)(2,1)} %get-tuple-element.16.kv_ref, bf16[2560,128]{1,0:T(8,128)(2,1)} %get-tuple-element.17.qg_ref, s32[20,128]{1,0:T(8,128)} %get-tuple-element.18.starts_ref, s32[1]{0:T(128)} %bitcast.2.base_ref), custom_call_target="tpu_custom_call" | custom-call | tf_op jit(solution)/shard_map/attend/pallas_call | solution.py:407
  107.1 49.0 %scatter_heads.1 = (bf16[160,1024]{1,0:T(8,128)(2,1)}, bf16[160,1024]{1,0:T(8,128)(2,1)}, bf16[160,1024]{1,0:T(8,128)(2,1)}, bf16[160,1024]{1,0:T(8,128)(2,1)}, f32[32,128]{1,0:T(8,128)}) custom-call(bf16[2560,128]{1,0:T(8,128)(2,1)} %get-tuple-element.19.oq_ref, bf16[4864,128]{1,0:T(8,128)(2,1)} %get-tuple-element.20.dkv_ref, bf16[160,1024]{1,0:T(8,128)(2,1)} %cot_ref.3, ...), custom_call_target="tpu_custom_call" | custom-call | tf_op jit(solution)/shard_map/scatter_heads/pallas_call | solution.py:425
  156.0 0.0 copy-start.1
  156.1 0.0 copy-start
  156.1 0.0 copy-start.2
  156.1 1.8 %copy.18 = bf16[160,1024]{1,0:T(8,128)(2,1)} copy(bf16[160,1024]{1,0:T(8,128)(2,1)} %get-tuple-element.32) | data formatting | bytes 655360
  157.9 1.7 %copy.19 = bf16[160,1024]{1,0:T(8,128)(2,1)} copy(bf16[160,1024]{1,0:T(8,128)(2,1)} %get-tuple-element.33) | data formatting | bytes 655360
  159.6 0.0 copy-done.1
  159.6 0.7 copy.20
  160.3 0.0 copy-done
  160.3 0.7 copy.21
  161.0 0.0 copy-done.2
  161.0 0.6 copy.22
  (2 shorter events, 0.0 us)
Async XLA Ops:
  156.0 3.5 %copy-start.1 = (bf16[160,1024]{1,0:T(8,128)(2,1)S(1)}, bf16[160,1024]{1,0:T(8,128)(2,1)}, u32[]{:S(2)}) copy-start(bf16[160,1024]{1,0:T(8,128)(2,1)} %get-tuple-element.34) | copy-start | bytes 983044
  156.1 4.2 %copy-start = (bf16[160,1024]{1,0:T(8,128)(2,1)S(1)}, bf16[160,1024]{1,0:T(8,128)(2,1)}, u32[]{:S(2)}) copy-start(bf16[160,1024]{1,0:T(8,128)(2,1)} %get-tuple-element.35) | copy-start | bytes 983044
  156.1 5.0 %copy-start.2 = (f32[32,128]{1,0:T(8,128)S(1)}, f32[32,128]{1,0:T(8,128)}, u32[]{:S(2)}) copy-start(f32[32,128]{1,0:T(8,128)} %get-tuple-element.26) | copy-start | bytes 49156

commit v2 on v1

v2 whole, which is shorter than its diff:
```python
import functools
import math

import jax
import jax.numpy as jnp
from jax import lax
from jax.experimental import pallas as pl
from jax.experimental.pallas import tpu as pltpu
from jax.sharding import PartitionSpec as P

D = 1024
HEADS = 16
HEAD = 64
WIN = 1120
RIM = 1120
TQ = 256
SPAN = 2496
CHUNKS = [(k, min(256, SPAN - k)) for k in range(0, SPAN, 256)]
FAR = -1e30
MESH = pl.DeviceIdType.MESH
BF16 = jnp.bfloat16
F32 = jnp.float32
VMEM_LIMIT = 56 * 1024 * 1024


def spot():
    me = lax.axis_index("seq")
    return me, me // HEADS, lax.rem(me, HEADS)


def push(src, dst, send, recv, device):
    return pltpu.make_async_remote_copy(
        src_ref=src, dst_ref=dst, send_sem=send, recv_sem=recv, device_id=(device,), device_id_type=MESH
    )


def lanes_low(shape):
    return lax.broadcasted_iota(jnp.int32, shape, 1) < HEAD


def pair_up(left, right, out):
    for k in range(HEADS // 2):
        cols = pl.ds(2 * HEAD * k, 2 * HEAD)
        a, b = left[:, cols], right[:, cols]
        out[2 * k] = jnp.concatenate([a[:, :HEAD], b[:, :HEAD]], axis=1)
        out[2 * k + 1] = jnp.concatenate([a[:, HEAD:], b[:, HEAD:]], axis=1)


def split_up(blocks, left, right):
    for k in range(HEADS // 2):
        cols = pl.ds(2 * HEAD * k, 2 * HEAD)
        a, b = blocks[2 * k], blocks[2 * k + 1]
        left[:, cols] = jnp.concatenate([a[:, :HEAD], b[:, :HEAD]], axis=1)
        right[:, cols] = jnp.concatenate([a[:, HEAD:], b[:, HEAD:]], axis=1)


def halves(ref):
    half = ref.shape[0] // 2
    return ref.at[pl.ds(0, half)], ref.at[pl.ds(half, half)]


def own_starts(len_ref, shift_ref, first_point, offset, all_points):
    count, points = len_ref.shape[1], shift_ref.shape[1]
    lens = jnp.concatenate([len_ref[...], jnp.zeros((1, 256 - count), jnp.int32)], axis=1)
    order = lax.broadcasted_iota(jnp.int32, (256, 256), 0)
    column = lax.broadcasted_iota(jnp.int32, (256, 256), 1)
    ends = jnp.sum(jnp.where(column <= order, lens, 0).astype(F32), axis=1, keepdims=True).astype(jnp.int32)
    lane = lax.broadcasted_iota(jnp.int32, (256, 256), 1)
    index = first_point + lane
    past = (ends <= index) & (order < count)
    row_first = jnp.max(jnp.where(past, jnp.broadcast_to(ends, (256, 256)), 0).astype(F32), axis=0, keepdims=True).astype(jnp.int32)
    shift = jnp.concatenate([shift_ref[...], jnp.zeros((1, 256 - points), jnp.int32)], axis=1)
    starts = jnp.clip(row_first - shift, 0, all_points - WIN)
    starts = jnp.where(lane[:1] < points, starts, 0)
    return pltpu.roll(jnp.broadcast_to(starts, (8, 256)), offset, 1)


def layer_kernel(
    rows, inverse_root,
    q_ref, k_ref, v_ref, cot_ref, w_ref, len_ref, shift_ref,
    out_ref, dq_recv, kv_back, dw_ref,
    kv_send, q_send, q_recv, g_send, g_recv, o_send, o_recv, dq_send,
    kv, qg, st_send, st_recv, starts, w_recv, w_wide, weight, grad,
    keys_t, values_t, acc, scores, probs, outs_t, shares, flows,
    mixed, terms, sib_recv, half_sum, peer_recv, flat, last_recv,
    rim_send, rim_recv, kv_sum,
    kv_ss, kv_rs, q_ss, q_rs, g_ss, g_rs, o_ss, o_rs, st_ss, st_rs, w_ss, w_rs,
    dq_ss, dq_rs, b_ss, b_rs, x_ss, x_rs, s_ss, s_rs, t_ss, t_rs, rim_ss, rim_rs, back_ss, back_rs, sib_ss, sib_rs,
    z_ss, z_rs,
):
    me, row, place = spot()
    core = lax.rem(me, 2)
    points = q_ref.shape[0]
    span = HEADS * points
    held = kv.shape[0]
    scale = 1.0 / math.sqrt(HEAD)
    fold = scale * math.log2(math.e)
    sibling = me + 1 - 2 * core
    near = range(HEADS - 1)
    far = range(rows - 1)
    goals = [lax.rem(place + i, HEADS) for i in range(1, HEADS)]
    mates = [row * HEADS + goal for goal in goals]
    peers = [lax.rem(row + i, rows) * HEADS + place for i in range(1, rows)]
    lower = lax.rem(row + rows - 1, rows) * HEADS + place
    upper = lax.rem(row + 1, rows) * HEADS + place

    def block(at, offset=0):
        return pl.ds(pl.multiple_of(offset + at * points, 16), points)

    barrier = pltpu.get_barrier_semaphore()
    for device in mates + peers:
        pl.semaphore_signal(barrier, inc=1, device_id=(device,), device_id_type=MESH)
    pair_up(k_ref, v_ref, kv_send)
    pair_up(*halves(q_ref), q_send)
    st_send[...] = own_starts(
        len_ref, shift_ref, me * points, lax.rem(place * points, 128), rows * span
    )
    pl.semaphore_wait(barrier, len(mates) + len(peers))

    part = w_ref.shape[0]
    w_at = pl.ds(pl.multiple_of(place * part, part), part)
    w_copies = [push(w_ref, w_recv.at[w_at], w_ss.at[i], w_rs.at[i], mates[i]) for i in near]
    kv_copies = [push(kv_send.at[goals[i]], kv.at[block(place, RIM)], kv_ss.at[i], kv_rs.at[i], mates[i]) for i in near]
    q_copies = [push(q_send.at[goals[i]], q_recv.at[place], q_ss.at[i], q_rs.at[i], mates[i]) for i in near]
    st_copies = [push(st_send, st_recv.at[place], st_ss.at[i], st_rs.at[i], mates[i]) for i in near]
    for copy in w_copies + kv_copies + st_copies + q_copies:
        copy.start()
    w_recv[w_at] = w_ref[...]
    kv[block(place, RIM), :] = kv_send[place]
    q_recv[place] = q_send[place]
    st_recv[place] = st_send[...]

    @pl.loop(0, held // 160)
    def _(t):
        acc[pl.ds(pl.multiple_of(t * 160, 160), 160), :] = jnp.zeros((160, 2 * HEAD), F32)

    values_t[HEAD:, :] = jnp.ones((16, values_t.shape[1]), BF16)

    for copy in w_copies:
        copy.wait_recv()
    w_wide[...] = w_recv[...].astype(F32)
    wrows = HEADS * part * 2 * HEAD // D
    half = wrows // 2
    own = pl.multiple_of(row * wrows, 16)
    for b in range(D // 128):
        weight[pl.ds(own, wrows), pl.ds(b * 128, 128)] = w_wide[pl.ds(b, wrows, stride=D // 128), :].astype(BF16)
    my_half = weight.at[pl.ds(pl.multiple_of(own + core * half, 16), half)]
    x_copies = [push(my_half, my_half, x_ss.at[i], x_rs.at[i], peers[i]) for i in far]
    for copy in x_copies:
        copy.start()

    for copy in kv_copies:
        copy.wait_recv()
    rim_copies = [
        push(kv.at[pl.ds(RIM, RIM)], kv.at[pl.ds(RIM + span, RIM)], rim_ss.at[0], rim_rs.at[0], lower),
        push(kv.at[pl.ds(span, RIM)], kv.at[pl.ds(0, RIM)], rim_ss.at[1], rim_rs.at[1], upper),
    ]
    for copy in rim_copies:
        copy.start()

    def turn(at, size):
        flipped = kv[pl.ds(at, size), :].astype(F32).T.astype(BF16)
        keys_t[:, pl.ds(at, size)] = flipped[:HEAD]
        values_t[:HEAD, pl.ds(at, size)] = flipped[HEAD:]

    inner = (-(-RIM // 128), (RIM + span) // 128)

    @pl.loop(*inner)
    def _(t):
        turn(pl.multiple_of(t * 128, 128), 128)

    t_copies = []
    for i in far:
        x_copies[i].wait_recv()
        source = lax.rem(row + rows - i - 1, rows)
        came = weight.at[pl.ds(pl.multiple_of(source * wrows + core * half, 16), half)]
        copy = push(came, came, t_ss.at[i], t_rs.at[i], sibling)
        copy.start()
        t_copies.append(copy)
    for copy in t_copies:
        copy.wait_recv()
    grad[...] = lax.dot_general(
        cot_ref[...], weight[...], (((1,), (1,)), ((), ())), preferred_element_type=F32
    ).astype(BF16)
    pair_up(*halves(grad), g_send)
    g_copies = [push(g_send.at[goals[i]], g_recv.at[place], g_ss.at[i], g_rs.at[i], mates[i]) for i in near]
    for copy in g_copies:
        copy.start()
    g_recv[place] = g_send[place]

    for copy in st_copies:
        copy.wait_recv()
    for t in range(span // 128):
        total = None
        for p in range(HEADS):
            first = p * points // 128
            if first <= t <= first + 1:
                piece = st_recv[p, 0:1, pl.ds((t - first) * 128, 128)]
                total = piece if total is None else total + piece
        starts[t // 2 : t // 2 + 1, (t % 2) * 128 : (t % 2 + 1) * 128] = total
    for copy in q_copies:
        copy.wait_recv()
    side = points // 2

    @pl.loop(0, HEADS)
    def _(p):
        a = q_recv[p]
        zero = jnp.zeros((side, HEAD), BF16)
        at = pl.multiple_of(p * points, 16)
        qg[pl.ds(at, side), :] = jnp.concatenate([a[:, :HEAD], zero], axis=1)
        qg[pl.ds(at + side, side), :] = jnp.concatenate([a[:, HEAD:], zero], axis=1)

    for copy in rim_copies:
        copy.wait_recv()

    @pl.loop(0, inner[0])
    def _(t):
        turn(pl.multiple_of(t * 128, 128), 128)

    @pl.loop(inner[1], held // 128)
    def _(t):
        turn(pl.multiple_of(t * 128, 128), 128)

    turn(held // 128 * 128, held % 128)

    base = row * span - RIM

    @pl.loop(0, span // TQ)
    def _(t):
        first = pl.multiple_of(t * TQ, TQ)
        query = qg[pl.ds(first, TQ), :]
        rel = starts[pl.ds(t, 1), :] - base - first
        top = jnp.full((8, TQ), FAR, F32)
        for k, n in CHUNKS:
            s = lax.dot_general(
                kv[pl.ds(first + k, n), :], query, (((1,), (1,)), ((), ())), preferred_element_type=F32
            )
            past = lax.broadcasted_iota(jnp.int32, (n, TQ), 0) - (rel - k)
            s = jnp.where((past >= 0) & (past < WIN), s, FAR)
            scores[pl.ds(k, n), :] = s
            top = jnp.maximum(top, jnp.max(s.reshape(n // 8, 8, TQ), axis=0))
        top = jnp.max(top, axis=0, keepdims=True)
        made = jnp.zeros((HEAD + 16, TQ), F32)
        for k, n in CHUNKS:
            p = jnp.exp2((scores[pl.ds(k, n), :] - top) * fold).astype(BF16)
            probs[t, pl.ds(k, n), :] = p
            made += jnp.dot(values_t[:, pl.ds(first + k, n)], p, preferred_element_type=F32)
        share = 1.0 / made[HEAD : HEAD + 1]
        shares[pl.ds(t, 1), :] = share
        out_t = made[:HEAD] * share
        outs_t[t] = out_t
        flows[pl.ds(first, TQ), :] = jnp.concatenate([out_t, out_t], axis=0).T.astype(BF16)

    @pl.loop(0, HEADS)
    def _(p):
        at = pl.multiple_of(p * points, 16)
        low, high = flows[pl.ds(at, side), :], flows[pl.ds(at + side, side), :]
        o_send[p] = jnp.concatenate([low[:, :HEAD], high[:, HEAD:]], axis=1)

    o_copies = [push(o_send.at[goals[i]], o_recv.at[place], o_ss.at[i], o_rs.at[i], mates[i]) for i in near]
    for copy in o_copies:
        copy.start()
    o_recv[place] = o_send[place]

    for copy in g_copies:
        copy.wait_recv()

    @pl.loop(0, HEADS)
    def _(p):
        a, b = q_recv[p], g_recv[p]
        at = pl.multiple_of(p * points, 16)
        qg[pl.ds(at, side), :] = jnp.concatenate([a[:, :HEAD], b[:, :HEAD]], axis=1)
        qg[pl.ds(at + side, side), :] = jnp.concatenate([a[:, HEAD:], b[:, HEAD:]], axis=1)

    def dq_copy(p):
        return push(dq_send.at[p], dq_recv.at[place], dq_ss.at[p], dq_rs.at[place], row * HEADS + p)

    def send_dq(p):
        at = pl.multiple_of(p * points, 16)
        low, high = flows[pl.ds(at, side), :], flows[pl.ds(at + side, side), :]
        dq_send[p] = jnp.concatenate([low[:, :HEAD], high[:, HEAD:]], axis=1)

        @pl.when(p != place)
        def _():
            dq_copy(p).start()

        @pl.when(p == place)
        def _():
            dq_recv[p] = dq_send[p]

    def back_copy(p):
        return push(kv_sum.at[block(p)], kv_back.at[place], b_ss.at[p], b_rs.at[place], row * HEADS + p)

    def send_back(p, rim, offset):
        value = acc[block(p, RIM), :]
        if rim is not None:
            value += rim_recv[rim, block(p, -offset), :].astype(F32)
        kv_sum[block(p), :] = value.astype(BF16)

        @pl.when(p != place)
        def _():
            back_copy(p).start()

        @pl.when(p == place)
        def _():
            kv_back[p] = kv_sum[block(p), :]

    rim_backs = [
        push(rim_send.at[0], rim_recv.at[1], back_ss.at[0], back_rs.at[0], lower),
        push(rim_send.at[1], rim_recv.at[0], back_ss.at[1], back_rs.at[1], upper),
    ]
    sib_copy = push(terms.at[1 - core], sib_recv, sib_ss, sib_rs, sibling)

    def to_sum(r):
        return pl.ds(pl.multiple_of(r * half, half), half)

    sum_ats = [to_sum(lax.rem(row + i, rows)) for i in range(rows)]
    s_copies = [push(half_sum.at[sum_ats[i + 1]], peer_recv.at[i], s_ss.at[i], s_rs.at[i], peers[i]) for i in far]
    place_in_half = place // 2
    z_goals = [core * (HEADS // 2) + j for j in range(HEADS // 2)]
    z_copies = [
        push(flat.at[pl.ds(j * part, part)], last_recv.at[place_in_half], z_ss.at[j], z_rs.at[place_in_half], row * HEADS + goal)
        for j, goal in enumerate(z_goals)
    ]

    low_lanes = lanes_low((TQ, 2 * HEAD))

    @pl.loop(0, span // TQ)
    def _(t):
        first = pl.multiple_of(t * TQ, TQ)
        query = qg[pl.ds(first, TQ), :]
        wide = query.astype(F32)
        slant = jnp.where(low_lanes, jnp.zeros_like(query), query)
        share = shares[pl.ds(t, 1), :]
        delta = jnp.sum(wide.T[HEAD:] * outs_t[t], axis=0, keepdims=True)
        scaled = wide * jnp.broadcast_to(share, (2 * HEAD, TQ)).T
        for_keys = jnp.where(low_lanes, scaled * scale, 0.0).astype(BF16)
        for_values = jnp.where(low_lanes, 0.0, scaled).astype(BF16)
        dq_t = jnp.zeros((HEAD, TQ), F32)
        for k, n in CHUNKS:
            turned = lax.dot_general(
                kv[pl.ds(first + k, n), :], slant, (((1,), (1,)), ((), ())), preferred_element_type=F32
            )
            p = probs[t, pl.ds(k, n), :]
            ds = p * (turned - delta).astype(BF16)
            dq_t += jnp.dot(keys_t[:, pl.ds(first + k, n)], ds, preferred_element_type=F32)
            acc[pl.ds(first + k, n), :] += jnp.dot(ds, for_keys, preferred_element_type=F32) + jnp.dot(
                p, for_values, preferred_element_type=F32
            )
        dq_t = dq_t * (share * scale)
        flows[pl.ds(first, TQ), :] = jnp.concatenate([dq_t, dq_t], axis=0).T.astype(BF16)

        @pl.when(t == 1)
        def _():
            for copy in o_copies:
                copy.wait_recv()
            split_up(o_recv, *halves(mixed))
            for k in range(HEADS // 2):
                term = lax.dot_general(
                    mixed[:, pl.ds(2 * HEAD * k, 2 * HEAD)], cot_ref[...], (((0,), (0,)), ((), ())),
                    preferred_element_type=F32,
                ).astype(BF16)
                for j in range(4):
                    terms[j % 2, pl.ds((2 * k + j // 2) * half, half), :] = term[j * half : (j + 1) * half]
            sib_copy.start()
            out_ref[...] = jnp.dot(mixed[...], weight[...], preferred_element_type=F32).astype(BF16)

        @pl.when(t == 2)
        def _():
            sib_copy.wait_recv()
            for i in range(rows):
                at = sum_ats[i]
                half_sum[at, :] = (terms[core, at, :].astype(F32) + sib_recv[at, :].astype(F32)).astype(BF16)
                if i:
                    s_copies[i - 1].start()

        @pl.when(t == 4)
        def _():
            rim_send[0] = acc[pl.ds(0, RIM), :].astype(BF16)
            rim_backs[0].start()
            for i in range(HEADS // 2):
                send_dq(lax.rem(place + i, HEADS // 2))

        @pl.when(t == 8)
        def _():
            total = half_sum[sum_ats[0], :].astype(F32)
            for i in far:
                s_copies[i].wait_recv()
                total += peer_recv[i].astype(F32)
            total = total * inverse_root
            for b in range(D // 128):
                flat[pl.ds(b, half, stride=D // 128), :] = total[:, b * 128 : (b + 1) * 128]
            for j, goal in enumerate(z_goals):

                @pl.when(goal != place)
                def _():
                    z_copies[j].start()

                @pl.when(goal == place)
                def _():
                    last_recv[place_in_half] = flat[pl.ds(j * part, part), :]

    rim_send[1] = acc[pl.ds(RIM + span, RIM), :].astype(BF16)
    rim_backs[1].start()
    rim_backs[0].wait_recv()
    free = RIM // points
    for i in range(HEADS - 2 * free):
        send_back(free + i, None, 0)
    for i in range(free):
        send_back(HEADS - free + lax.rem(place + i, free), 1, span - RIM)
    for i in range(HEADS // 2):
        send_dq(HEADS // 2 + lax.rem(place + i, HEADS // 2))
    rim_backs[1].wait_recv()
    for i in range(free):
        send_back(lax.rem(place + i, free), 0, 0)

    for z in range(HEADS // 2):
        source = 2 * z + place // (HEADS // 2)

        @pl.when(source != place)
        def _():
            push(flat.at[pl.ds(0, part)], last_recv.at[z], z_ss.at[0], z_rs.at[z], row * HEADS + source).wait_recv()

    dw_ref[...] = jnp.sum(last_recv[...], axis=0)

    for p in range(HEADS):

        @pl.when(p != place)
        def _():
            push(dq_send.at[p], dq_recv.at[p], dq_ss.at[p], dq_rs.at[p], row * HEADS + p).wait_recv()
            push(kv_sum.at[block(p)], kv_back.at[p], b_ss.at[p], b_rs.at[p], row * HEADS + p).wait_recv()
            dq_copy(p).wait_send()
            back_copy(p).wait_send()

    for goal, copy in zip(z_goals, z_copies, strict=True):

        @pl.when(goal != place)
        def _():
            copy.wait_send()

    for copies in (
        w_copies, kv_copies, st_copies, q_copies, x_copies, t_copies, rim_copies, g_copies, o_copies,
        rim_backs, [sib_copy], s_copies,
    ):
        for copy in copies:
            copy.wait_send()


def unpack_kernel(out_in, dq_in, kv_in, dw_in, out_ref, dq_ref, dk_ref, dv_ref, dw_ref):
    out_ref[...] = out_in[...]
    dw_ref[...] = dw_in[...]
    split_up(dq_in, *halves(dq_ref))
    split_up(kv_in, dk_ref, dv_ref)


def in_vmem(count):
    return [pl.BlockSpec(memory_space=pltpu.VMEM)] * count


def per_device(queries, key_rows, value_rows, out_weight, cotangent, row_lengths, window_shift):
    points = queries.shape[0]
    devices = lax.axis_size("seq")
    rows = devices // HEADS
    span = HEADS * points
    held = span + 2 * RIM
    tiles = span // TQ
    lanes = -(-held // 128) * 128
    w_part = out_weight.shape[0] // 128
    wide = 2 * HEAD
    half = HEAD // 2
    dma = pltpu.SemaphoreType.DMA
    ring, all_row, cross = dma((HEADS - 1,)), dma((HEADS,)), dma((rows - 1,))
    full = jax.ShapeDtypeStruct((points, D), BF16)
    sums = jax.ShapeDtypeStruct((w_part, 128), F32)
    blocks = pltpu.VMEM((HEADS, points, wide), BF16)
    packed = pltpu.VMEM((HEADS, points // 2, wide), BF16)
    made = pl.pallas_call(
        functools.partial(layer_kernel, rows, 1.0 / math.sqrt(devices * points)),
        out_shape=(
            full,
            jax.ShapeDtypeStruct((HEADS, points // 2, wide), BF16),
            jax.ShapeDtypeStruct((HEADS, points, wide), BF16),
            sums,
        ),
        in_specs=in_vmem(7),
        out_specs=tuple(in_vmem(4)),
        scratch_shapes=[
            blocks, packed, packed, packed, packed, packed, packed, packed,
            pltpu.VMEM((held, wide), BF16),
            pltpu.VMEM((span, wide), BF16),
            pltpu.VMEM((8, 256), jnp.int32),
            pltpu.VMEM((HEADS, 8, 256), jnp.int32),
            pltpu.VMEM((tiles, TQ), jnp.int32),
            pltpu.VMEM((HEADS * w_part, 128), BF16),
            pltpu.VMEM((HEADS * w_part, 128), F32),
            pltpu.VMEM((D, D), BF16),
            pltpu.VMEM((points, D), BF16),
            pltpu.VMEM((HEAD, lanes), BF16),
            pltpu.VMEM((HEAD + 16, lanes), BF16),
            pltpu.VMEM((held, wide), F32),
            pltpu.VMEM((SPAN, TQ), F32),
            pltpu.VMEM((tiles, SPAN, TQ), BF16),
            pltpu.VMEM((tiles, HEAD, TQ), F32),
            pltpu.VMEM((tiles, TQ), F32),
            pltpu.VMEM((span, wide), BF16),
            pltpu.VMEM((points, D), BF16),
            pltpu.VMEM((2, rows * half, D), BF16),
            pltpu.VMEM((rows * half, D), BF16),
            pltpu.VMEM((rows * half, D), BF16),
            pltpu.VMEM((rows - 1, half, D), BF16),
            pltpu.VMEM((half * D // 128, 128), F32),
            pltpu.VMEM((HEADS // 2, w_part, 128), F32),
            pltpu.VMEM((2, RIM, wide), BF16),
            pltpu.VMEM((2, RIM, wide), BF16),
            pltpu.VMEM((span, wide), BF16),
            ring, ring, ring, ring, ring, ring, ring, ring, ring, ring, ring, ring,
            all_row, all_row, all_row, all_row, cross, cross, cross, cross, cross, cross,
            dma((2,)), dma((2,)), dma((2,)), dma((2,)), dma, dma,
            dma((HEADS // 2,)), dma((HEADS // 2,)),
        ],
        compiler_params=pltpu.CompilerParams(
            collective_id=0, has_side_effects=True, vmem_limit_bytes=VMEM_LIMIT
        ),
        name="layer",
    )(
        queries, key_rows, value_rows, cotangent, out_weight.reshape(w_part, 128),
        row_lengths.reshape(1, -1), window_shift.reshape(1, -1),
    )
    out, dq, dk, dv, dw = pl.pallas_call(
        unpack_kernel,
        out_shape=(full, full, full, full, sums),
        in_specs=in_vmem(4),
        out_specs=tuple(in_vmem(5)),
        compiler_params=pltpu.CompilerParams(vmem_limit_bytes=VMEM_LIMIT),
        name="unpack",
    )(*made)
    return (out, dq, dk, dv, dw.reshape(-1))


def solution(mesh):
    whole = P("seq", None)
    return jax.shard_map(
        per_device,
        mesh=mesh,
        in_specs=(whole, whole, whole, P("seq"), whole, P(), P("seq")),
        out_specs=(whole, whole, whole, whole, P("seq")),
        check_vma=False,
    )
```

time: 162 us -> 129 us (0.80)
  Pallas kernels: 152 us -> 128 us
  local copies, waits for them, and re-layouts: 6.39 us -> 0 us
  other arithmetic: 2.35 us -> 0 us
    pallas_call x3 -> x2, Pallas kernels: 152 us -> 128 us  [the longest x1 125 us: per_device(): pl.pallas_call(functools.partial(layer_kernel, rows, 1.0 / math.sqrt(devi...]
    unnamed x11 -> x0, local copies, waits for them, and re-layouts: 5.56 us -> none
    reduce_sum x2 -> x0, other arithmetic: 1.66 us -> none  [the longest x1 0.87 us: window_starts(): row_first = jnp.sum(jnp.where(passed, row_lengths[None, :], 0), axis=1)]
where the time goes in v2:
time: 129 us
  Pallas kernels  128 us (99%)
    pallas_call x1, Pallas kernels, per_device(): pl.pallas_call(functools.partial(layer_kernel, rows, 1.0 / math.sqrt(devi...  125 us

profile of v2, /device:TPU:25, one launch (start us, length us, event | category | flops | bytes accessed | tf_op | source)
XLA Modules:
  0.0 128.5 jit_solution(13296086401574204631)
XLA Ops:
  0.6 125.4 %layer.1 = (bf16[160,1024]{1,0:T(8,128)(2,1)}, bf16[16,80,128]{2,1,0:T(8,128)(2,1)}, bf16[16,160,128]{2,1,0:T(8,128)(2,1)}, f32[32,128]{1,0:T(8,128)}) custom-call(bf16[160,1024]{1,0:T(8,128)(2,1)} %q_ref.1, bf16[160,1024]{1,0:T(8,128)(2,1)} %k_ref.1, bf16[160,1024]{1,0:T(8,128)(2,1)} %v_ref.1, bf16[160,1024]{1,0:T(8,128)(2,1)} %cot_ref.1, ...), custom_call_target="tpu_custom_call" | custom-call | tf_op jit(solution)/shard_map/layer/pallas_call | solution.py:477
  126.0 2.6 %unpack.1 = (bf16[160,1024]{1,0:T(8,128)(2,1)}, bf16[160,1024]{1,0:T(8,128)(2,1)}, bf16[160,1024]{1,0:T(8,128)(2,1)}, bf16[160,1024]{1,0:T(8,128)(2,1)}, f32[32,128]{1,0:T(8,128)}) custom-call(bf16[160,1024]{1,0:T(8,128)(2,1)} %get-tuple-element.14.out_in, bf16[16,80,128]{2,1,0:T(8,128)(2,1)} %get-tuple-element.15.dq_in, ...), custom_call_target="tpu_custom_call" | custom-call | tf_op jit(solution)/shard_map/unpack/pallas_call | solution.py:529

commit v3 on v2

--- a/solution.py
+++ b/solution.py
@@ -16,6 +16,7 @@
 TQ = 256
 SPAN = 2496
 CHUNKS = [(k, min(256, SPAN - k)) for k in range(0, SPAN, 256)]
+LONG_CHUNKS = [(k, min(1280, SPAN - k)) for k in range(0, SPAN, 1280)]
 FAR = -1e30
 MESH = pl.DeviceIdType.MESH
 BF16 = jnp.bfloat16
@@ -77,22 +78,24 @@
 
 def layer_kernel(
     rows, inverse_root,
-    q_ref, k_ref, v_ref, cot_ref, w_ref, len_ref, shift_ref,
+    q_in, k_in, v_in, cot_in, w_ref, len_ref, shift_ref,
     out_ref, dq_recv, kv_back, dw_ref,
-    kv_send, q_send, q_recv, g_send, g_recv, o_send, o_recv, dq_send,
-    kv, qg, st_send, st_recv, starts, w_recv, w_wide, weight, grad,
+    q_ref, k_ref, v_ref, cot_ref,
+    kq_send, v_send, v_recv, g_send, g_recv, o_send, o_recv, dq_send,
+    v_rims, kq, vals, qg, st_send, st_recv, starts, w_recv, w_wide, weight, grad,
     keys_t, values_t, acc, scores, probs, outs_t, shares, flows,
     mixed, terms, sib_recv, half_sum, peer_recv, flat, last_recv,
     rim_send, rim_recv, kv_sum,
-    kv_ss, kv_rs, q_ss, q_rs, g_ss, g_rs, o_ss, o_rs, st_ss, st_rs, w_ss, w_rs,
-    dq_ss, dq_rs, b_ss, b_rs, x_ss, x_rs, s_ss, s_rs, t_ss, t_rs, rim_ss, rim_rs, back_ss, back_rs, sib_ss, sib_rs,
+    in_sems,
+    kv_ss, kv_rs, v_ss, v_rs, g_ss, g_rs, o_ss, o_rs, st_ss, st_rs, w_ss, w_rs,
+    dq_ss, dq_rs, b_ss, b_rs, x_ss, x_rs, s_ss, s_rs, t_ss, t_rs, rim_ss, rim_rs, vr_ss, vr_rs, back_ss, back_rs, sib_ss, sib_rs,
     z_ss, z_rs,
 ):
     me, row, place = spot()
     core = lax.rem(me, 2)
     points = q_ref.shape[0]
     span = HEADS * points
-    held = kv.shape[0]
+    held = kq.shape[0]
     scale = 1.0 / math.sqrt(HEAD)
     fold = scale * math.log2(math.e)
     sibling = me + 1 - 2 * core
@@ -110,31 +113,38 @@
     barrier = pltpu.get_barrier_semaphore()
     for device in mates + peers:
         pl.semaphore_signal(barrier, inc=1, device_id=(device,), device_id_type=MESH)
-    pair_up(k_ref, v_ref, kv_send)
-    pair_up(*halves(q_ref), q_send)
+    loads = [
+        pltpu.make_async_copy(src, dst, in_sems.at[i])
+        for i, (src, dst) in enumerate(((k_in, k_ref), (q_in, q_ref), (v_in, v_ref), (cot_in, cot_ref)))
+    ]
+    for copy in loads:
+        copy.start()
+    loads[0].wait()
+    loads[1].wait()
+    pair_up(k_ref, q_ref, kq_send)
+    pl.semaphore_wait(barrier, len(mates) + len(peers))
+
+    part = w_ref.shape[0]
+    w_at = pl.ds(pl.multiple_of(place * part, part), part)
+    w_copies = [push(w_ref, w_recv.at[w_at], w_ss.at[i], w_rs.at[i], mates[i]) for i in near]
+    kv_copies = [push(kq_send.at[goals[i]], kq.at[block(place, RIM)], kv_ss.at[i], kv_rs.at[i], mates[i]) for i in near]
+    v_copies = [push(v_send.at[goals[i]], v_recv.at[place], v_ss.at[i], v_rs.at[i], mates[i]) for i in near]
+    st_copies = [push(st_send, st_recv.at[place], st_ss.at[i], st_rs.at[i], mates[i]) for i in near]
+    for copy in w_copies + kv_copies:
+        copy.start()
+    loads[2].wait()
+    pair_up(*halves(v_ref), v_send)
+    for copy in v_copies:
+        copy.start()
     st_send[...] = own_starts(
         len_ref, shift_ref, me * points, lax.rem(place * points, 128), rows * span
     )
-    pl.semaphore_wait(barrier, len(mates) + len(peers))
-
-    part = w_ref.shape[0]
-    w_at = pl.ds(pl.multiple_of(place * part, part), part)
-    w_copies = [push(w_ref, w_recv.at[w_at], w_ss.at[i], w_rs.at[i], mates[i]) for i in near]
-    kv_copies = [push(kv_send.at[goals[i]], kv.at[block(place, RIM)], kv_ss.at[i], kv_rs.at[i], mates[i]) for i in near]
-    q_copies = [push(q_send.at[goals[i]], q_recv.at[place], q_ss.at[i], q_rs.at[i], mates[i]) for i in near]
-    st_copies = [push(st_send, st_recv.at[place], st_ss.at[i], st_rs.at[i], mates[i]) for i in near]
-    for copy in w_copies + kv_copies + st_copies + q_copies:
+    for copy in st_copies:
         copy.start()
     w_recv[w_at] = w_ref[...]
-    kv[block(place, RIM), :] = kv_send[place]
-    q_recv[place] = q_send[place]
+    kq[block(place, RIM), :] = kq_send[place]
+    v_recv[place] = v_send[place]
     st_recv[place] = st_send[...]
-
-    @pl.loop(0, held // 160)
-    def _(t):
-        acc[pl.ds(pl.multiple_of(t * 160, 160), 160), :] = jnp.zeros((160, 2 * HEAD), F32)
-
-    values_t[HEAD:, :] = jnp.ones((16, values_t.shape[1]), BF16)
 
     for copy in w_copies:
         copy.wait_recv()
@@ -149,44 +159,67 @@
     for copy in x_copies:
         copy.start()
 
-    for copy in kv_copies:
-        copy.wait_recv()
-    rim_copies = [
-        push(kv.at[pl.ds(RIM, RIM)], kv.at[pl.ds(RIM + span, RIM)], rim_ss.at[0], rim_rs.at[0], lower),
-        push(kv.at[pl.ds(span, RIM)], kv.at[pl.ds(0, RIM)], rim_ss.at[1], rim_rs.at[1], upper),
-    ]
-    for copy in rim_copies:
-        copy.start()
+    @pl.loop(0, held // 160)
+    def _(t):
+        acc[pl.ds(pl.multiple_of(t * 160, 160), 160), :] = jnp.zeros((160, 2 * HEAD), F32)
+
+    values_t[HEAD:, :] = jnp.ones((16, values_t.shape[1]), BF16)
+
+    rim_blocks = RIM // points
+
+    def rim_down(p):
+        return push(kq.at[block(p, RIM)], kq.at[block(p, RIM + span)], rim_ss.at[p], rim_rs.at[p], lower)
+
+    def rim_up(p):
+        at = p - (HEADS - rim_blocks)
+        return push(kq.at[block(p, RIM)], kq.at[block(at)], rim_ss.at[p], rim_rs.at[p], upper)
+
+    def rim_on(p):
+        @pl.when(p < rim_blocks)
+        def _():
+            rim_down(p).start()
+
+        @pl.when(p >= HEADS - rim_blocks)
+        def _():
+            rim_up(p).start()
+
+    rim_on(place)
+    for i in near:
+        kv_copies[i].wait_recv()
+        rim_on(lax.rem(place + HEADS - i - 1, HEADS))
+    rim_copies = [rim_down(p) for p in range(rim_blocks)] + [rim_up(p) for p in range(HEADS - rim_blocks, HEADS)]
+
+    side = points // 2
+
+    def v_down(p):
+        return push(v_recv.at[p], v_rims.at[p + rim_blocks], vr_ss.at[p], vr_rs.at[p], lower)
+
+    def v_up(p):
+        return push(v_recv.at[p], v_rims.at[p - (HEADS - rim_blocks)], vr_ss.at[p], vr_rs.at[p], upper)
+
+    def v_on(p):
+        @pl.when(p < rim_blocks)
+        def _():
+            v_down(p).start()
+
+        @pl.when(p >= HEADS - rim_blocks)
+        def _():
+            v_up(p).start()
+
+    v_rim_copies = [v_down(p) for p in range(rim_blocks)] + [v_up(p) for p in range(HEADS - rim_blocks, HEADS)]
+
+    def lay_values(packed, at):
+        vals[pl.ds(at, side), :] = packed[:, :HEAD]
+        vals[pl.ds(at + side, side), :] = packed[:, HEAD:]
 
     def turn(at, size):
-        flipped = kv[pl.ds(at, size), :].astype(F32).T.astype(BF16)
-        keys_t[:, pl.ds(at, size)] = flipped[:HEAD]
-        values_t[:HEAD, pl.ds(at, size)] = flipped[HEAD:]
-
-    inner = (-(-RIM // 128), (RIM + span) // 128)
-
-    @pl.loop(*inner)
-    def _(t):
-        turn(pl.multiple_of(t * 128, 128), 128)
-
-    t_copies = []
-    for i in far:
-        x_copies[i].wait_recv()
-        source = lax.rem(row + rows - i - 1, rows)
-        came = weight.at[pl.ds(pl.multiple_of(source * wrows + core * half, 16), half)]
-        copy = push(came, came, t_ss.at[i], t_rs.at[i], sibling)
-        copy.start()
-        t_copies.append(copy)
-    for copy in t_copies:
-        copy.wait_recv()
-    grad[...] = lax.dot_general(
-        cot_ref[...], weight[...], (((1,), (1,)), ((), ())), preferred_element_type=F32
-    ).astype(BF16)
-    pair_up(*halves(grad), g_send)
+        keys_t[:, pl.ds(at, size)] = kq[pl.ds(at, size), :].astype(F32).T[:HEAD].astype(BF16)
+        values_t[:HEAD, pl.ds(at, size)] = vals[pl.ds(at, size), :].astype(F32).T.astype(BF16)
+
+    sources = [lax.rem(row + rows - i - 1, rows) for i in far]
+    came = [weight.at[pl.ds(pl.multiple_of(r * wrows + core * half, 16), half)] for r in sources]
+    t_copies = [push(came[i], came[i], t_ss.at[i], t_rs.at[i], sibling) for i in far]
     g_copies = [push(g_send.at[goals[i]], g_recv.at[place], g_ss.at[i], g_rs.at[i], mates[i]) for i in near]
-    for copy in g_copies:
-        copy.start()
-    g_recv[place] = g_send[place]
 
     for copy in st_copies:
         copy.wait_recv()
@@ -198,79 +231,122 @@
                 piece = st_recv[p, 0:1, pl.ds((t - first) * 128, 128)]
                 total = piece if total is None else total + piece
         starts[t // 2 : t // 2 + 1, (t % 2) * 128 : (t % 2 + 1) * 128] = total
-    for copy in q_copies:
-        copy.wait_recv()
-    side = points // 2
-
-    @pl.loop(0, HEADS)
-    def _(p):
-        a = q_recv[p]
-        zero = jnp.zeros((side, HEAD), BF16)
-        at = pl.multiple_of(p * points, 16)
-        qg[pl.ds(at, side), :] = jnp.concatenate([a[:, :HEAD], zero], axis=1)
-        qg[pl.ds(at + side, side), :] = jnp.concatenate([a[:, HEAD:], zero], axis=1)
-
     for copy in rim_copies:
         copy.wait_recv()
 
-    @pl.loop(0, inner[0])
-    def _(t):
-        turn(pl.multiple_of(t * 128, 128), 128)
-
-    @pl.loop(inner[1], held // 128)
-    def _(t):
-        turn(pl.multiple_of(t * 128, 128), 128)
-
-    turn(held // 128 * 128, held % 128)
-
     base = row * span - RIM
+    tiles = span // TQ
+    half_row = HEADS // 2
+
+    def o_copy(p):
+        return push(o_send.at[p], o_recv.at[place], o_ss.at[p], o_rs.at[place], row * HEADS + p)
+
+    def send_o(p):
+        at = pl.multiple_of(p * points, 16)
+        low, high = flows[pl.ds(at, side), :], flows[pl.ds(at + side, side), :]
+        o_send[p] = jnp.concatenate([low[:, :HEAD], high[:, HEAD:]], axis=1)
+
+        @pl.when(p != place)
+        def _():
+            o_copy(p).start()
+
+        @pl.when(p == place)
+        def _():
+            o_recv[p] = o_send[p]
 
     @pl.loop(0, span // TQ)
     def _(t):
         first = pl.multiple_of(t * TQ, TQ)
-        query = qg[pl.ds(first, TQ), :]
+        query = kq[pl.ds(pl.multiple_of(first + RIM, 16), TQ), HEAD:]
+        query = jnp.concatenate([query, jnp.zeros_like(query)], axis=1)
         rel = starts[pl.ds(t, 1), :] - base - first
         top = jnp.full((8, TQ), FAR, F32)
         for k, n in CHUNKS:
             s = lax.dot_general(
-                kv[pl.ds(first + k, n), :], query, (((1,), (1,)), ((), ())), preferred_element_type=F32
+                kq[pl.ds(first + k, n), :], query, (((1,), (1,)), ((), ())), preferred_element_type=F32
             )
             past = lax.broadcasted_iota(jnp.int32, (n, TQ), 0) - (rel - k)
-            s = jnp.where((past >= 0) & (past < WIN), s, FAR)
+            s = jnp.where(past.astype(jnp.uint32) < jnp.uint32(WIN), s, FAR)
             scores[pl.ds(k, n), :] = s
             top = jnp.maximum(top, jnp.max(s.reshape(n // 8, 8, TQ), axis=0))
         top = jnp.max(top, axis=0, keepdims=True)
-        made = jnp.zeros((HEAD + 16, TQ), F32)
         for k, n in CHUNKS:
-            p = jnp.exp2((scores[pl.ds(k, n), :] - top) * fold).astype(BF16)
-            probs[t, pl.ds(k, n), :] = p
-            made += jnp.dot(values_t[:, pl.ds(first + k, n)], p, preferred_element_type=F32)
+            probs[t, pl.ds(k, n), :] = jnp.exp2((scores[pl.ds(k, n), :] - top) * fold).astype(BF16)
+
+        @pl.when(t == 1)
+        def _():
+            for i in far:
+                x_copies[i].wait_recv()
+                t_copies[i].start()
+
+        @pl.when(t == 4)
+        def _():
+            for copy in t_copies:
+                copy.wait_recv()
+            loads[3].wait()
+            grad[...] = lax.dot_general(
+                cot_ref[...], weight[...], (((1,), (1,)), ((), ())), preferred_element_type=F32
+            ).astype(BF16)
+            pair_up(*halves(grad), g_send)
+            for copy in g_copies:
+                copy.start()
+            g_recv[place] = g_send[place]
+
+        @pl.when(t == 3)
+        def _():
+            v_on(place)
+            for i in near:
+                v_copies[i].wait_recv()
+                v_on(lax.rem(place + HEADS - i - 1, HEADS))
+
+    @pl.loop(0, HEADS)
+    def _(p):
+        lay_values(v_recv[p], pl.multiple_of(RIM + p * points, 16))
+
+    for copy in v_rim_copies:
+        copy.wait_recv()
+
+    @pl.loop(0, rim_blocks)
+    def _(p):
+        lay_values(v_rims[p], pl.multiple_of(p * points, 16))
+        lay_values(v_rims[p + rim_blocks], pl.multiple_of(RIM + span + p * points, 16))
+
+    @pl.loop(0, held // 128)
+    def _(t):
+        turn(pl.multiple_of(t * 128, 128), 128)
+
+    turn(held // 128 * 128, held % 128)
+
+    @pl.loop(0, span // TQ)
+    def _(step):
+        t = lax.rem(step + core * (tiles // 2), tiles)
+        first = pl.multiple_of(t * TQ, TQ)
+        made = jnp.dot(values_t[:, pl.ds(first, SPAN)], probs[t], preferred_element_type=F32)
         share = 1.0 / made[HEAD : HEAD + 1]
         shares[pl.ds(t, 1), :] = share
         out_t = made[:HEAD] * share
         outs_t[t] = out_t
         flows[pl.ds(first, TQ), :] = jnp.concatenate([out_t, out_t], axis=0).T.astype(BF16)
 
+        @pl.when(step == tiles // 2 - 1)
+        def _():
+            for i in range(half_row):
+                send_o(core * half_row + lax.rem(place + i, half_row))
+
+    for i in range(half_row):
+        send_o((1 - core) * half_row + lax.rem(place + i, half_row))
+
+    for copy in g_copies:
+        copy.wait_recv()
+
     @pl.loop(0, HEADS)
     def _(p):
+        b = g_recv[p]
         at = pl.multiple_of(p * points, 16)
-        low, high = flows[pl.ds(at, side), :], flows[pl.ds(at + side, side), :]
-        o_send[p] = jnp.concatenate([low[:, :HEAD], high[:, HEAD:]], axis=1)
-
-    o_copies = [push(o_send.at[goals[i]], o_recv.at[place], o_ss.at[i], o_rs.at[i], mates[i]) for i in near]
-    for copy in o_copies:
-        copy.start()
-    o_recv[place] = o_send[place]
-
-    for copy in g_copies:
-        copy.wait_recv()
-
-    @pl.loop(0, HEADS)
-    def _(p):
-        a, b = q_recv[p], g_recv[p]
-        at = pl.multiple_of(p * points, 16)
-        qg[pl.ds(at, side), :] = jnp.concatenate([a[:, :HEAD], b[:, :HEAD]], axis=1)
-        qg[pl.ds(at + side, side), :] = jnp.concatenate([a[:, HEAD:], b[:, HEAD:]], axis=1)
+        low = kq[pl.ds(pl.multiple_of(at + RIM, 16), side), HEAD:]
+        high = kq[pl.ds(pl.multiple_of(at + side + RIM, 16), side), HEAD:]
+        qg[pl.ds(at, side), :] = jnp.concatenate([low, b[:, :HEAD]], axis=1)
+        qg[pl.ds(at + side, side), :] = jnp.concatenate([high, b[:, HEAD:]], axis=1)
 
     def dq_copy(p):
         return push(dq_send.at[p], dq_recv.at[place], dq_ss.at[p], dq_rs.at[place], row * HEADS + p)
@@ -291,10 +367,10 @@
     def back_copy(p):
         return push(kv_sum.at[block(p)], kv_back.at[place], b_ss.at[p], b_rs.at[place], row * HEADS + p)
 
-    def send_back(p, rim, offset):
+    def send_back(p, rim, at):
         value = acc[block(p, RIM), :]
         if rim is not None:
-            value += rim_recv[rim, block(p, -offset), :].astype(F32)
+            value += rim_recv[rim, block(at), :].astype(F32)
         kv_sum[block(p), :] = value.astype(BF16)
 
         @pl.when(p != place)
@@ -305,10 +381,17 @@
         def _():
             kv_back[p] = kv_sum[block(p), :]
 
+    towards = lower + core * (upper - lower)
     rim_backs = [
-        push(rim_send.at[0], rim_recv.at[1], back_ss.at[0], back_rs.at[0], lower),
-        push(rim_send.at[1], rim_recv.at[0], back_ss.at[1], back_rs.at[1], upper),
+        push(rim_send.at[0], rim_recv.at[1 - core], back_ss.at[0], back_rs.at[0], towards),
+        push(rim_send.at[1], rim_recv.at[core], back_ss.at[1], back_rs.at[1], lower + upper - towards),
     ]
+
+    def send_rim(i, side_of_row):
+        at = pl.multiple_of(side_of_row * (RIM + span), 16)
+        rim_send[i] = acc[pl.ds(at, RIM), :].astype(BF16)
+        rim_backs[i].start()
+
     sib_copy = push(terms.at[1 - core], sib_recv, sib_ss, sib_rs, sibling)
 
     def to_sum(r):
@@ -326,20 +409,21 @@
     low_lanes = lanes_low((TQ, 2 * HEAD))
 
     @pl.loop(0, span // TQ)
-    def _(t):
+    def _(step):
+        t = lax.rem(step + core * (tiles // 2), tiles)
         first = pl.multiple_of(t * TQ, TQ)
         query = qg[pl.ds(first, TQ), :]
         wide = query.astype(F32)
-        slant = jnp.where(low_lanes, jnp.zeros_like(query), query)
+        slant = query[:, HEAD:]
         share = shares[pl.ds(t, 1), :]
         delta = jnp.sum(wide.T[HEAD:] * outs_t[t], axis=0, keepdims=True)
         scaled = wide * jnp.broadcast_to(share, (2 * HEAD, TQ)).T
         for_keys = jnp.where(low_lanes, scaled * scale, 0.0).astype(BF16)
         for_values = jnp.where(low_lanes, 0.0, scaled).astype(BF16)
         dq_t = jnp.zeros((HEAD, TQ), F32)
-        for k, n in CHUNKS:
+        for k, n in LONG_CHUNKS:
             turned = lax.dot_general(
-                kv[pl.ds(first + k, n), :], slant, (((1,), (1,)), ((), ())), preferred_element_type=F32
+                vals[pl.ds(first + k, n), :], slant, (((1,), (1,)), ((), ())), preferred_element_type=F32
             )
             p = probs[t, pl.ds(k, n), :]
             ds = p * (turned - delta).astype(BF16)
@@ -350,10 +434,14 @@
         dq_t = dq_t * (share * scale)
         flows[pl.ds(first, TQ), :] = jnp.concatenate([dq_t, dq_t], axis=0).T.astype(BF16)
 
-        @pl.when(t == 1)
-        def _():
-            for copy in o_copies:
-                copy.wait_recv()
+        @pl.when(step == 5)
+        def _():
+            for p in range(HEADS):
+
+                @pl.when(p != place)
+                def _():
+                    push(o_send.at[p], o_recv.at[p], o_ss.at[p], o_rs.at[p], row * HEADS + p).wait_recv()
+
             split_up(o_recv, *halves(mixed))
             for k in range(HEADS // 2):
                 term = lax.dot_general(
@@ -365,54 +453,52 @@
             sib_copy.start()
             out_ref[...] = jnp.dot(mixed[...], weight[...], preferred_element_type=F32).astype(BF16)
 
-        @pl.when(t == 2)
+        @pl.when(step == 8)
         def _():
             sib_copy.wait_recv()
             for i in range(rows):
                 at = sum_ats[i]
                 half_sum[at, :] = (terms[core, at, :].astype(F32) + sib_recv[at, :].astype(F32)).astype(BF16)
-                if i:
-                    s_copies[i - 1].start()
-
-        @pl.when(t == 4)
-        def _():
-            rim_send[0] = acc[pl.ds(0, RIM), :].astype(BF16)
-            rim_backs[0].start()
-            for i in range(HEADS // 2):
-                send_dq(lax.rem(place + i, HEADS // 2))
-
-        @pl.when(t == 8)
-        def _():
-            total = half_sum[sum_ats[0], :].astype(F32)
-            for i in far:
-                s_copies[i].wait_recv()
-                total += peer_recv[i].astype(F32)
-            total = total * inverse_root
-            for b in range(D // 128):
-                flat[pl.ds(b, half, stride=D // 128), :] = total[:, b * 128 : (b + 1) * 128]
-            for j, goal in enumerate(z_goals):
-
-                @pl.when(goal != place)
-                def _():
-                    z_copies[j].start()
-
-                @pl.when(goal == place)
-                def _():
-                    last_recv[place_in_half] = flat[pl.ds(j * part, part), :]
-
-    rim_send[1] = acc[pl.ds(RIM + span, RIM), :].astype(BF16)
-    rim_backs[1].start()
+
+        @pl.when(step == 4)
+        def _():
+            send_rim(0, core)
+            for i in range(half_row):
+                send_dq(core * half_row + lax.rem(place + i, half_row))
+
+    send_rim(1, 1 - core)
+    for copy in s_copies:
+        copy.start()
+    for i in range(half_row):
+        send_dq((1 - core) * half_row + lax.rem(place + i, half_row))
+    free = rim_blocks
+    for i in range(HEADS - 2 * free):
+        send_back(free + i, None, None)
     rim_backs[0].wait_recv()
-    free = RIM // points
-    for i in range(HEADS - 2 * free):
-        send_back(free + i, None, 0)
     for i in range(free):
-        send_back(HEADS - free + lax.rem(place + i, free), 1, span - RIM)
-    for i in range(HEADS // 2):
-        send_dq(HEADS // 2 + lax.rem(place + i, HEADS // 2))
+        at = lax.rem(place + i, free)
+        send_back((1 - core) * (HEADS - free) + at, 1 - core, at)
     rim_backs[1].wait_recv()
     for i in range(free):
-        send_back(lax.rem(place + i, free), 0, 0)
+        at = lax.rem(place + i, free)
+        send_back(core * (HEADS - free) + at, core, at)
+
+    total = half_sum[sum_ats[0], :].astype(F32)
+    for i in far:
+        s_copies[i].wait_recv()
+        total += peer_recv[i].astype(F32)
+    total = total * inverse_root
+    for b in range(D // 128):
+        flat[pl.ds(b, half, stride=D // 128), :] = total[:, b * 128 : (b + 1) * 128]
+    for j, goal in enumerate(z_goals):
+
+        @pl.when(goal != place)
+        def _():
+            z_copies[j].start()
+
+        @pl.when(goal == place)
+        def _():
+            last_recv[place_in_half] = flat[pl.ds(j * part, part), :]
 
     for z in range(HEADS // 2):
         source = 2 * z + place // (HEADS // 2)
@@ -430,6 +516,7 @@
             push(dq_send.at[p], dq_recv.at[p], dq_ss.at[p], dq_rs.at[p], row * HEADS + p).wait_recv()
             push(kv_sum.at[block(p)], kv_back.at[p], b_ss.at[p], b_rs.at[p], row * HEADS + p).wait_recv()
             dq_copy(p).wait_send()
+            o_copy(p).wait_send()
             back_copy(p).wait_send()
 
     for goal, copy in zip(z_goals, z_copies, strict=True):
@@ -439,7 +526,7 @@
             copy.wait_send()
 
     for copies in (
-        w_copies, kv_copies, st_copies, q_copies, x_copies, t_copies, rim_copies, g_copies, o_copies,
+        w_copies, kv_copies, st_copies, v_copies, x_copies, t_copies, rim_copies, v_rim_copies, g_copies,
         rim_backs, [sib_copy], s_copies,
     ):
         for copy in copies:
@@ -455,6 +542,10 @@
 
 def in_vmem(count):
     return [pl.BlockSpec(memory_space=pltpu.VMEM)] * count
+
+
+def anywhere(count):
+    return [pl.BlockSpec(memory_space=pl.ANY)] * count
 
 
 def per_device(queries, key_rows, value_rows, out_weight, cotangent, row_lengths, window_shift):
@@ -471,6 +562,7 @@
     dma = pltpu.SemaphoreType.DMA
     ring, all_row, cross = dma((HEADS - 1,)), dma((HEADS,)), dma((rows - 1,))
     full = jax.ShapeDtypeStruct((points, D), BF16)
+    own = pltpu.VMEM((points, D), BF16)
     sums = jax.ShapeDtypeStruct((w_part, 128), F32)
     blocks = pltpu.VMEM((HEADS, points, wide), BF16)
     packed = pltpu.VMEM((HEADS, points // 2, wide), BF16)
@@ -482,11 +574,14 @@
             jax.ShapeDtypeStruct((HEADS, points, wide), BF16),
             sums,
         ),
-        in_specs=in_vmem(7),
+        in_specs=anywhere(4) + in_vmem(3),
         out_specs=tuple(in_vmem(4)),
         scratch_shapes=[
+            own, own, own, own,
             blocks, packed, packed, packed, packed, packed, packed, packed,
+            pltpu.VMEM((2 * RIM // points, points // 2, wide), BF16),
             pltpu.VMEM((held, wide), BF16),
+            pltpu.VMEM((held, HEAD), BF16),
             pltpu.VMEM((span, wide), BF16),
             pltpu.VMEM((8, 256), jnp.int32),
             pltpu.VMEM((HEADS, 8, 256), jnp.int32),
@@ -513,9 +608,10 @@
             pltpu.VMEM((2, RIM, wide), BF16),
             pltpu.VMEM((2, RIM, wide), BF16),
             pltpu.VMEM((span, wide), BF16),
-            ring, ring, ring, ring, ring, ring, ring, ring, ring, ring, ring, ring,
+            dma((4,)),
+            ring, ring, ring, ring, ring, ring, all_row, all_row, ring, ring, ring, ring,
             all_row, all_row, all_row, all_row, cross, cross, cross, cross, cross, cross,
-            dma((2,)), dma((2,)), dma((2,)), dma((2,)), dma, dma,
+            all_row, all_row, all_row, all_row, dma((2,)), dma((2,)), dma, dma,
             dma((HEADS // 2,)), dma((HEADS // 2,)),
         ],
         compiler_params=pltpu.CompilerParams(

time: 129 us -> 118 us (0.915)
  the two profiles are of different devices: /device:TPU:25 before, /device:TPU:11 now
where the time goes in v3:
time: 118 us
  Pallas kernels  117 us (99%)
    pallas_call x1, Pallas kernels, per_device(): pl.pallas_call(functools.partial(layer_kernel, rows, 1.0 / math.sqrt(devi...  115 us
    pallas_call x1, Pallas kernels, per_device(): pl.pallas_call(unpack_kernel, out_shape=(full, full, full, full, sums), i...  2.55 us

profile of v3, /device:TPU:11, one launch (start us, length us, event | category | flops | bytes accessed | tf_op | source)
XLA Modules:
  0.0 117.9 jit_solution(9293433965426163101)
XLA Ops:
  0.6 114.7 %layer.1 = (bf16[160,1024]{1,0:T(8,128)(2,1)}, bf16[16,80,128]{2,1,0:T(8,128)(2,1)}, bf16[16,160,128]{2,1,0:T(8,128)(2,1)}, f32[32,128]{1,0:T(8,128)}) custom-call(bf16[160,1024]{1,0:T(8,128)(2,1)} %q_in.1, bf16[160,1024]{1,0:T(8,128)(2,1)} %k_in.1, bf16[160,1024]{1,0:T(8,128)(2,1)} %v_in.1, bf16[160,1024]{1,0:T(8,128)(2,1)} %cot_in.1, ...), custom_call_target="tpu_custom_call" | custom-call | tf_op jit(solution)/shard_map/layer/pallas_call | solution.py:569
  115.4 2.6 %unpack.1 = (bf16[160,1024]{1,0:T(8,128)(2,1)}, bf16[160,1024]{1,0:T(8,128)(2,1)}, bf16[160,1024]{1,0:T(8,128)(2,1)}, bf16[160,1024]{1,0:T(8,128)(2,1)}, f32[32,128]{1,0:T(8,128)}) custom-call(bf16[160,1024]{1,0:T(8,128)(2,1)} %get-tuple-element.14.out_in, bf16[16,80,128]{2,1,0:T(8,128)(2,1)} %get-tuple-element.15.dq_in, ...), custom_call_target="tpu_custom_call" | custom-call | tf_op jit(solution)/shard_map/unpack/pallas_call | solution.py:625

commit v4 on v3

--- a/solution.py
+++ b/solution.py
@@ -93,6 +93,7 @@
 ):
     me, row, place = spot()
     core = lax.rem(me, 2)
+    back = lax.rem(core + row, 2)
     points = q_ref.shape[0]
     span = HEADS * points
     held = kq.shape[0]
@@ -319,7 +320,7 @@
 
     @pl.loop(0, span // TQ)
     def _(step):
-        t = lax.rem(step + core * (tiles // 2), tiles)
+        t = step + back * (tiles - 1 - 2 * step)
         first = pl.multiple_of(t * TQ, TQ)
         made = jnp.dot(values_t[:, pl.ds(first, SPAN)], probs[t], preferred_element_type=F32)
         share = 1.0 / made[HEAD : HEAD + 1]
@@ -331,10 +332,10 @@
         @pl.when(step == tiles // 2 - 1)
         def _():
             for i in range(half_row):
-                send_o(core * half_row + lax.rem(place + i, half_row))
+                send_o(back * half_row + lax.rem(place + i, half_row))
 
     for i in range(half_row):
-        send_o((1 - core) * half_row + lax.rem(place + i, half_row))
+        send_o((1 - back) * half_row + lax.rem(place + i, half_row))
 
     for copy in g_copies:
         copy.wait_recv()
@@ -381,16 +382,20 @@
         def _():
             kv_back[p] = kv_sum[block(p), :]
 
-    towards = lower + core * (upper - lower)
-    rim_backs = [
-        push(rim_send.at[0], rim_recv.at[1 - core], back_ss.at[0], back_rs.at[0], towards),
-        push(rim_send.at[1], rim_recv.at[core], back_ss.at[1], back_rs.at[1], lower + upper - towards),
-    ]
+    towards = lower + back * (upper - lower)
+    away = lower + upper - towards
+
+    def rim_back(i, b):
+        slot, device = (back, away) if i else (1 - back, towards)
+        at = i * rim_blocks + b
+        return push(rim_send.at[i, block(b)], rim_recv.at[slot, block(b)], back_ss.at[at], back_rs.at[at], device)
+
+    rim_backs = [rim_back(i, b) for i in range(2) for b in range(rim_blocks)]
 
     def send_rim(i, side_of_row):
-        at = pl.multiple_of(side_of_row * (RIM + span), 16)
-        rim_send[i] = acc[pl.ds(at, RIM), :].astype(BF16)
-        rim_backs[i].start()
+        for b in range(rim_blocks):
+            rim_send[i, block(b), :] = acc[block(b, side_of_row * (RIM + span)), :].astype(BF16)
+            rim_back(i, b).start()
 
     sib_copy = push(terms.at[1 - core], sib_recv, sib_ss, sib_rs, sibling)
 
@@ -406,11 +411,19 @@
         for j, goal in enumerate(z_goals)
     ]
 
+    free = rim_blocks
+
+    def send_first(i):
+        p = i + back * (HEADS - 1 - 2 * i)
+        at = p - back * (HEADS - free)
+        rim_back(0, at).wait_recv()
+        send_back(p, back, at)
+
     low_lanes = lanes_low((TQ, 2 * HEAD))
 
     @pl.loop(0, span // TQ)
     def _(step):
-        t = lax.rem(step + core * (tiles // 2), tiles)
+        t = step + back * (tiles - 1 - 2 * step)
         first = pl.multiple_of(t * TQ, TQ)
         query = qg[pl.ds(first, TQ), :]
         wide = query.astype(F32)
@@ -462,26 +475,31 @@
 
         @pl.when(step == 4)
         def _():
-            send_rim(0, core)
+            send_rim(0, back)
             for i in range(half_row):
-                send_dq(core * half_row + lax.rem(place + i, half_row))
-
-    send_rim(1, 1 - core)
+                send_dq(back * half_row + lax.rem(place + i, half_row))
+
+        @pl.when(step == 7)
+        def _():
+            for i in range(5):
+                send_first(lax.rem(place + i, 5))
+
+        @pl.when(step == 8)
+        def _():
+            for i in range(2):
+                send_first(5 + lax.rem(place + i, 2))
+
+    send_rim(1, 1 - back)
+    for i in range(half_row):
+        send_dq((1 - back) * half_row + lax.rem(place + i, half_row))
+    for i in range(HEADS - 2 * free):
+        send_back(free + i, None, None)
     for copy in s_copies:
         copy.start()
-    for i in range(half_row):
-        send_dq((1 - core) * half_row + lax.rem(place + i, half_row))
-    free = rim_blocks
-    for i in range(HEADS - 2 * free):
-        send_back(free + i, None, None)
-    rim_backs[0].wait_recv()
     for i in range(free):
         at = lax.rem(place + i, free)
-        send_back((1 - core) * (HEADS - free) + at, 1 - core, at)
-    rim_backs[1].wait_recv()
-    for i in range(free):
-        at = lax.rem(place + i, free)
-        send_back(core * (HEADS - free) + at, core, at)
+        rim_back(1, at).wait_recv()
+        send_back((1 - back) * (HEADS - free) + at, 1 - back, at)
 
     total = half_sum[sum_ats[0], :].astype(F32)
     for i in far:
@@ -611,7 +629,7 @@
             dma((4,)),
             ring, ring, ring, ring, ring, ring, all_row, all_row, ring, ring, ring, ring,
             all_row, all_row, all_row, all_row, cross, cross, cross, cross, cross, cross,
-            all_row, all_row, all_row, all_row, dma((2,)), dma((2,)), dma, dma,
+            all_row, all_row, all_row, all_row, dma((2 * (RIM // points),)), dma((2 * (RIM // points),)), dma, dma,
             dma((HEADS // 2,)), dma((HEADS // 2,)),
         ],
         compiler_params=pltpu.CompilerParams(

time: 118 us -> 117 us (level)
  the two profiles are of different devices: /device:TPU:11 before, /device:TPU:25 now
where the time goes in v4:
time: 117 us; the launch traced here: 116 us
  Pallas kernels  116 us (99%)
    pallas_call x1, Pallas kernels, per_device(): pl.pallas_call(functools.partial(layer_kernel, rows, 1.0 / math.sqrt(devi...  113 us
    pallas_call x1, Pallas kernels, per_device(): pl.pallas_call(unpack_kernel, out_shape=(full, full, full, full, sums), i...  2.55 us

profile of v4, /device:TPU:25, one launch (start us, length us, event | category | flops | bytes accessed | tf_op | source)
XLA Modules:
  0.0 116.4 jit_solution(15074016320702477929)
XLA Ops:
  0.6 113.3 %layer.1 = (bf16[160,1024]{1,0:T(8,128)(2,1)}, bf16[16,80,128]{2,1,0:T(8,128)(2,1)}, bf16[16,160,128]{2,1,0:T(8,128)(2,1)}, f32[32,128]{1,0:T(8,128)}) custom-call(bf16[160,1024]{1,0:T(8,128)(2,1)} %q_in.1, bf16[160,1024]{1,0:T(8,128)(2,1)} %k_in.1, bf16[160,1024]{1,0:T(8,128)(2,1)} %v_in.1, bf16[160,1024]{1,0:T(8,128)(2,1)} %cot_in.1, ...), custom_call_target="tpu_custom_call" | custom-call | tf_op jit(solution)/shard_map/layer/pallas_call | solution.py:587
  113.9 2.6 %unpack.1 = (bf16[160,1024]{1,0:T(8,128)(2,1)}, bf16[160,1024]{1,0:T(8,128)(2,1)}, bf16[160,1024]{1,0:T(8,128)(2,1)}, bf16[160,1024]{1,0:T(8,128)(2,1)}, f32[32,128]{1,0:T(8,128)}) custom-call(bf16[160,1024]{1,0:T(8,128)(2,1)} %get-tuple-element.14.out_in, bf16[16,80,128]{2,1,0:T(8,128)(2,1)} %get-tuple-element.15.dq_in, ...), custom_call_target="tpu_custom_call" | custom-call | tf_op jit(solution)/shard_map/unpack/pallas_call | solution.py:643

commit v5 on v4

--- a/solution.py
+++ b/solution.py
@@ -131,7 +131,7 @@
     kv_copies = [push(kq_send.at[goals[i]], kq.at[block(place, RIM)], kv_ss.at[i], kv_rs.at[i], mates[i]) for i in near]
     v_copies = [push(v_send.at[goals[i]], v_recv.at[place], v_ss.at[i], v_rs.at[i], mates[i]) for i in near]
     st_copies = [push(st_send, st_recv.at[place], st_ss.at[i], st_rs.at[i], mates[i]) for i in near]
-    for copy in w_copies + kv_copies:
+    for copy in kv_copies + w_copies:
         copy.start()
     loads[2].wait()
     pair_up(*halves(v_ref), v_send)

time: 117 us -> 131 us (1.12)
  Pallas kernels: 116 us -> 130 us
    pallas_call x1, Pallas kernels: 113 us -> 127 us  [per_device(): pl.pallas_call(functools.partial(layer_kernel, rows, 1.0 / math.sqrt(devi...]
where the time goes in v5:
time: 131 us; the launch traced here: 130 us
  Pallas kernels  130 us (99%)
    pallas_call x1, Pallas kernels, per_device(): pl.pallas_call(functools.partial(layer_kernel, rows, 1.0 / math.sqrt(devi...  127 us

profile of v5, /device:TPU:25, one launch (start us, length us, event | category | flops | bytes accessed | tf_op | source)
XLA Modules:
  0.0 130.2 jit_solution(12652449200529863264)
XLA Ops:
  0.6 127.0 %layer.1 = (bf16[160,1024]{1,0:T(8,128)(2,1)}, bf16[16,80,128]{2,1,0:T(8,128)(2,1)}, bf16[16,160,128]{2,1,0:T(8,128)(2,1)}, f32[32,128]{1,0:T(8,128)}) custom-call(bf16[160,1024]{1,0:T(8,128)(2,1)} %q_in.1, bf16[160,1024]{1,0:T(8,128)(2,1)} %k_in.1, bf16[160,1024]{1,0:T(8,128)(2,1)} %v_in.1, bf16[160,1024]{1,0:T(8,128)(2,1)} %cot_in.1, ...), custom_call_target="tpu_custom_call" | custom-call | tf_op jit(solution)/shard_map/layer/pallas_call | solution.py:587
  127.6 2.6 %unpack.1 = (bf16[160,1024]{1,0:T(8,128)(2,1)}, bf16[160,1024]{1,0:T(8,128)(2,1)}, bf16[160,1024]{1,0:T(8,128)(2,1)}, bf16[160,1024]{1,0:T(8,128)(2,1)}, f32[32,128]{1,0:T(8,128)}) custom-call(bf16[160,1024]{1,0:T(8,128)(2,1)} %get-tuple-element.14.out_in, bf16[16,80,128]{2,1,0:T(8,128)(2,1)} %get-tuple-element.15.dq_in, ...), custom_call_target="tpu_custom_call" | custom-call | tf_op jit(solution)/shard_map/unpack/pallas_call | solution.py:643
